TPU v7x, 256 devices: a whole 4x4x8 slice. The times are simulated.
256 devices in a mesh: ctx: 32 (over y_lo, z, core), tp: 8 (over x, y_hi).
Axes of the slice: x: 4, y: 4 (y_hi: 2, y_lo: 2; y = y_hi * 2 + y_lo), z: 8, core: 2. Of those that a mesh axis runs over, the one named last changes fastest.
Arguments:
- query_act: bfloat16 [8192, 8192], P('ctx', 'tp'), may hold values from -6 to 6
- key_act: bfloat16 [8192, 1024], P('ctx', 'tp'), may hold values from -6 to 6
- value_act: bfloat16 [8192, 1024], P('ctx', 'tp'), may hold values from -6 to 6
- attn_out: bfloat16 [8192, 8192], P('ctx', 'tp'), may hold values from -6 to 6
- d_out: bfloat16 [8192, 8192], P('ctx', 'tp'), may hold values from -6 to 6
- log_norm: float32 [64, 8192], P('tp', 'ctx'), may hold values from 0 to 12
- span_order: int32 [64], replicated, may hold values from 0 to 63, as said below
- hidden: bfloat16 [8192, 5120], P('ctx'), may hold values from -0.0625 to 0.0625
- w_key: bfloat16 [5120, 1024], P(None, 'tp'), may hold values from -0.078125 to 0.078125
- w_value: bfloat16 [5120, 1024], P(None, 'tp'), may hold values from -0.078125 to 0.078125
Outputs:
- d_query: bfloat16 [8192, 8192], P('ctx', 'tp')
- d_key: bfloat16 [8192, 1024], P('ctx', 'tp')
- d_value: bfloat16 [8192, 1024], P('ctx', 'tp')
- grad_w_key: float32 [5120, 1024], P('ctx', 'tp')
- grad_w_value: float32 [5120, 1024], P('ctx', 'tp')
- d_hidden: bfloat16 [8192, 5120], P('ctx', 'tp')
Inputs may be any that keep to these rules, and one draw needn't show every extreme that they name: `span_order`: storage spans 2 i and 2 i + 1 hold the sequence spans i and 63 - i, in either order.
All inputs are finite; a program needn't handle non-finite values.
Results may differ from a plain program's by a relative error of at most 0.015.
Values may be sent and summed in bfloat16 or wider, within the bound.
A program may use at most 64 MiB of HBM per device.

v0:
```python
import math

import jax
import jax.numpy as jnp
from jax import lax
from jax.sharding import PartitionSpec as P

HEADS = 64
KV_HEADS = 8
HEAD_DIM = 128


def shifted(value, axis, steps):
    count = lax.axis_size(axis)
    pairs = [(source, (source + steps) % count) for source in range(count)]
    return lax.ppermute(value, axis, pairs)


def tile_grads(q_tile, grad_tile, norm_tile, delta_tile, key_tile, value_tile, q_pos, k_pos):
    score_scale = 1.0 / math.sqrt(HEAD_DIM)
    scores = (
        jnp.einsum("qhgd,khd->hgqk", q_tile, key_tile, preferred_element_type=jnp.float32)
        * score_scale
    )
    visible = k_pos[None, None, None, :] <= q_pos[None, None, :, None]
    probs = jnp.where(visible, jnp.exp(scores - norm_tile[..., None]), jnp.float32(0.0))
    dprobs = jnp.einsum("qhgd,khd->hgqk", grad_tile, value_tile, preferred_element_type=jnp.float32)
    dscores_low = (probs * (dprobs - delta_tile[..., None])).astype(jnp.bfloat16)
    probs_low = probs.astype(jnp.bfloat16)
    d_vals = jnp.einsum("hgqk,qhgd->khd", probs_low, grad_tile, preferred_element_type=jnp.float32)
    d_keys = (
        jnp.einsum("hgqk,qhgd->khd", dscores_low, q_tile, preferred_element_type=jnp.float32)
        * score_scale
    )
    d_quer = (
        jnp.einsum("hgqk,khd->qhgd", dscores_low, key_tile, preferred_element_type=jnp.float32)
        * score_scale
    )
    return (d_quer, d_keys, d_vals)


def pass_grads(grad_pair):
    return shifted(grad_pair, "ctx", 1)


def shards(
    query_act, key_act, value_act, attn_out, d_out, log_norm, span_order, hidden, w_key, w_value
):
    tok_rows = query_act.shape[0]
    span_len = tok_rows // 2
    kv_width = key_act.shape[1]
    kv_heads = kv_width // HEAD_DIM
    group_size = HEADS // KV_HEADS
    cycle_size = lax.axis_size("ctx")
    cycle_index = lax.axis_index("ctx")
    queries = query_act.reshape(tok_rows, kv_heads, group_size, HEAD_DIM)
    grads_in = d_out.reshape(tok_rows, kv_heads, group_size, HEAD_DIM)
    outputs = attn_out.reshape(tok_rows, kv_heads, group_size, HEAD_DIM)
    deltas = jnp.transpose(
        jnp.sum(grads_in.astype(jnp.float32) * outputs.astype(jnp.float32), axis=-1), (1, 2, 0)
    )
    norms = log_norm.reshape(kv_heads, group_size, tok_rows)
    own_spans = lax.dynamic_slice_in_dim(span_order, 2 * cycle_index, 2)
    offsets = jnp.arange(span_len, dtype=jnp.int32)
    q_pos_own = jnp.concatenate(
        [own_spans[0] * span_len + offsets, own_spans[1] * span_len + offsets]
    )

    def block_update(dq_acc, key_rows, value_rows, k_pos):
        rows_in = key_rows.shape[0]
        key_heads = key_rows.reshape(rows_in, kv_heads, HEAD_DIM)
        value_heads = value_rows.reshape(rows_in, kv_heads, HEAD_DIM)
        d_quer, d_keys, d_vals = tile_grads(
            queries, grads_in, norms, deltas, key_heads, value_heads, q_pos_own, k_pos
        )
        return (
            dq_acc + d_quer,
            d_keys.reshape(rows_in, kv_width),
            d_vals.reshape(rows_in, kv_width),
        )

    dq_start = jnp.zeros((tok_rows, kv_heads, group_size, HEAD_DIM), jnp.float32)

    def step_work(step_num, dq_acc, key_block, value_block, dk_run, dv_run):
        source = (cycle_index - step_num) % cycle_size
        source_spans = lax.dynamic_slice_in_dim(span_order, 2 * source, 2)
        k_pos = jnp.concatenate(
            [source_spans[0] * span_len + offsets, source_spans[1] * span_len + offsets]
        )
        dq_acc, dk_part, dv_part = block_update(dq_acc, key_block, value_block, k_pos)
        return (dq_acc, dk_run + dk_part, dv_run + dv_part)

    def cycle_step(step_num, state):
        dq_acc, key_block, value_block, dk_run, dv_run = state
        key_next, value_next = shifted((key_block, value_block), "ctx", 1)
        dq_acc, dk_run, dv_run = step_work(step_num, dq_acc, key_block, value_block, dk_run, dv_run)
        dk_run, dv_run = pass_grads((dk_run, dv_run))
        return (dq_acc, key_next, value_next, dk_run, dv_run)

    zero_grads = jnp.zeros((tok_rows, kv_width), jnp.float32)
    dq_acc, key_block, value_block, dk_run, dv_run = lax.fori_loop(
        0, cycle_size - 1, cycle_step, (dq_start, key_act, value_act, zero_grads, zero_grads)
    )
    dq_acc, dk_run, dv_run = step_work(
        cycle_size - 1, dq_acc, key_block, value_block, dk_run, dv_run
    )
    dk_mine, dv_mine = pass_grads((dk_run, dv_run))
    d_query = dq_acc.reshape(tok_rows, -1).astype(jnp.bfloat16)
    d_key = dk_mine.astype(jnp.bfloat16)
    d_value = dv_mine.astype(jnp.bfloat16)
    kv_grads = jnp.concatenate([d_key, d_value], axis=1)
    w_share = lax.psum_scatter(
        lax.dot_general(
            hidden, kv_grads, (((0,), (0,)), ((), ())), preferred_element_type=jnp.float32
        ),
        "ctx",
        scatter_dimension=0,
        tiled=True,
    )
    grad_w_key = w_share[:, :kv_width]
    grad_w_value = w_share[:, kv_width:]
    input_term = lax.dot_general(
        d_key, w_key, (((1,), (1,)), ((), ())), preferred_element_type=jnp.float32
    )
    input_term = input_term + lax.dot_general(
        d_value, w_value, (((1,), (1,)), ((), ())), preferred_element_type=jnp.float32
    )
    d_hidden = lax.psum_scatter(
        input_term.astype(jnp.bfloat16), "tp", scatter_dimension=1, tiled=True
    )
    return (d_query, d_key, d_value, grad_w_key, grad_w_value, d_hidden)


def solution(mesh):
    in_specs = (
        P("ctx", "tp"),
        P("ctx", "tp"),
        P("ctx", "tp"),
        P("ctx", "tp"),
        P("ctx", "tp"),
        P("tp", "ctx"),
        P(),
        P("ctx", None),
        P(None, "tp"),
        P(None, "tp"),
    )
    out_specs = (
        P("ctx", "tp"),
        P("ctx", "tp"),
        P("ctx", "tp"),
        P("ctx", "tp"),
        P("ctx", "tp"),
        P("ctx", "tp"),
    )
    return jax.shard_map(shards, mesh=mesh, in_specs=in_specs, out_specs=out_specs, check_vma=False)
```

profile of v0, /device:TPU:8, one launch (start us, length us, event | category | flops | bytes accessed | tf_op | source)
XLA Modules:
  0.0 744.8 jit_solution(4375925429317715415)
XLA Ops:
  25.0 488.9 %while.25 = (s32[]{:T(128)}, f32[256,1,8,128]{3,0,2,1:T(8,128)}, bf16[256,128]{1,0:T(8,128)(2,1)}, bf16[256,128]{1,0:T(8,128)(2,1)}, f32[256,128]{1,0:T(8,128)S(...) while((s32[]{:T(128)}, f32[256,1,8,128]{3,0,2,1:T(8,128)}, ...), condition=%wide.region_2.3_spmd.clone.clone, body=%wide.region_1.2_spmd.clone.clone.sunk | while | flops 675709440 | bytes 22632064 | solution.py:101
  37.7 2.7 fusion.99
  51.4 3.0 collective-permute-start.3
  54.4 3.0 fusion.99
  70.6 3.0 fusion.99
  86.0 3.0 fusion.99
  100.7 3.0 fusion.99
  115.5 3.0 fusion.99
  131.1 3.0 fusion.99
  134.1 2.6 collective-permute-done.2
  146.7 3.0 fusion.99
  162.4 3.0 fusion.99
  165.4 2.6 collective-permute-done.2
  178.1 3.0 fusion.99
  193.7 3.0 fusion.99
  196.7 2.6 collective-permute-done.2
  209.4 3.0 fusion.99
  225.0 3.0 fusion.99
  240.7 3.0 fusion.99
  256.3 3.0 fusion.99
  259.4 2.6 collective-permute-done.2
  272.0 3.0 fusion.99
  287.7 3.0 fusion.99
  290.7 2.6 collective-permute-done.2
  303.3 3.0 fusion.99
  319.0 3.0 fusion.99
  322.0 2.6 collective-permute-done.2
  334.6 3.0 fusion.99
  350.3 3.0 fusion.99
  366.0 3.0 fusion.99
  381.6 3.0 fusion.99
  384.6 2.6 collective-permute-done.2
  397.3 3.0 fusion.99
  412.9 3.0 fusion.99
  415.9 2.6 collective-permute-done.2
  428.6 3.0 fusion.99
  444.3 3.0 fusion.99
  447.3 2.6 collective-permute-done.2
  459.9 3.0 fusion.99
  475.6 3.0 fusion.99
  491.2 3.0 fusion.99
  506.9 3.0 fusion.99
  518.3 3.6 collective-permute-done.5
  526.5 4.4 copy.65
  531.0 3.2 convolution_bitcast_fusion.2
  534.2 5.9 copy.63
  545.6 64.2 %reduce-scatter.9.cloned.1.call-done = bf16[640,256]{1,0:T(8,128)(2,1)} async-done(((bf16[5120,256]{1,0:T(8,128)(2,1)}), bf16[640,256]{1,0:T(8,128)(2,1)}) %reduce-scatter.9.cloned.1.call-update) | async-done | bytes 327696
  611.7 123.5 %reduce-scatter.7.cloned.1.call-done = f32[160,256]{1,0:T(8,128)} async-done(((f32[5120,256]{1,0:T(8,128)}), f32[160,256]{1,0:T(8,128)}) %reduce-scatter.7.cloned.1.call-update) | async-done | bytes 163856
  (759 shorter events, 361.8 us)
Async XLA Ops:
  7.2 602.6 %reduce-scatter.9.cloned.1.call-start = ((), (), s32[]{:S(2)}) async-start(), calls=%async_computation.3 | async-start | bytes 2949120
  25.9 14.5 %collective-permute-start = (bf16[256,128]{1,0:T(8,128)(2,1)S(1)}, bf16[256,128]{1,0:T(8,128)(2,1)}, u32[]{:S(2)}, u32[]{:S(2)}) collective-permute-start(bf16[256,128]{1,0:T(8,128)(2,1)S(1)} %copy.95), channel_id=1, source_target_pairs={{0,8},{8,16},{16,24},{24,32},{32,40},{40,48},{48,56},{56,64},{64,7... | collective-permute-start | bytes 196616 | tf_op jit(solution)/shard_map/while/body/eval_jaxpr/ppermute | solution.py:16
  26.7 13.7 %collective-permute-start.1 = (bf16[256,128]{1,0:T(8,128)(2,1)S(1)}, bf16[256,128]{1,0:T(8,128)(2,1)}, u32[]{:S(2)}, u32[]{:S(2)}) collective-permute-start(bf16[256,128]{1,0:T(8,128)(2,1)S(1)} %copy.96), channel_id=1, source_target_pairs={{0,8},{8,16},{16,24},{24,32},{32,40},{40,48},{48,56},{56,64},{64,7... | collective-permute-start | bytes 196616 | tf_op jit(solution)/shard_map/while/body/eval_jaxpr/ppermute | solution.py:16
  43.6 13.8 %collective-permute-start = (bf16[256,128]{1,0:T(8,128)(2,1)S(1)}, bf16[256,128]{1,0:T(8,128)(2,1)}, u32[]{:S(2)}, u32[]{:S(2)}) collective-permute-start(bf16[256,128]{1,0:T(8,128)(2,1)S(1)} %copy.95), channel_id=1, source_target_pairs={{0,8},{8,16},{16,24},{24,32},{32,40},{40,48},{48,56},{56,64},{64,7... | collective-permute-start | bytes 196616 | tf_op jit(solution)/shard_map/while/body/eval_jaxpr/ppermute | solution.py:16
  44.4 13.0 %collective-permute-start.1 = (bf16[256,128]{1,0:T(8,128)(2,1)S(1)}, bf16[256,128]{1,0:T(8,128)(2,1)}, u32[]{:S(2)}, u32[]{:S(2)}) collective-permute-start(bf16[256,128]{1,0:T(8,128)(2,1)S(1)} %copy.96), channel_id=1, source_target_pairs={{0,8},{8,16},{16,24},{24,32},{32,40},{40,48},{48,56},{56,64},{64,7... | collective-permute-start | bytes 196616 | tf_op jit(solution)/shard_map/while/body/eval_jaxpr/ppermute | solution.py:16
  59.2 14.3 %collective-permute-start = (bf16[256,128]{1,0:T(8,128)(2,1)S(1)}, bf16[256,128]{1,0:T(8,128)(2,1)}, u32[]{:S(2)}, u32[]{:S(2)}) collective-permute-start(bf16[256,128]{1,0:T(8,128)(2,1)S(1)} %copy.95), channel_id=1, source_target_pairs={{0,8},{8,16},{16,24},{24,32},{32,40},{40,48},{48,56},{56,64},{64,7... | collective-permute-start | bytes 196616 | tf_op jit(solution)/shard_map/while/body/eval_jaxpr/ppermute | solution.py:16
  60.1 13.5 %collective-permute-start.1 = (bf16[256,128]{1,0:T(8,128)(2,1)S(1)}, bf16[256,128]{1,0:T(8,128)(2,1)}, u32[]{:S(2)}, u32[]{:S(2)}) collective-permute-start(bf16[256,128]{1,0:T(8,128)(2,1)S(1)} %copy.96), channel_id=1, source_target_pairs={{0,8},{8,16},{16,24},{24,32},{32,40},{40,48},{48,56},{56,64},{64,7... | collective-permute-start | bytes 196616 | tf_op jit(solution)/shard_map/while/body/eval_jaxpr/ppermute | solution.py:16
  76.1 12.9 %collective-permute-start = (bf16[256,128]{1,0:T(8,128)(2,1)S(1)}, bf16[256,128]{1,0:T(8,128)(2,1)}, u32[]{:S(2)}, u32[]{:S(2)}) collective-permute-start(bf16[256,128]{1,0:T(8,128)(2,1)S(1)} %copy.95), channel_id=1, source_target_pairs={{0,8},{8,16},{16,24},{24,32},{32,40},{40,48},{48,56},{56,64},{64,7... | collective-permute-start | bytes 196616 | tf_op jit(solution)/shard_map/while/body/eval_jaxpr/ppermute | solution.py:16
  76.9 12.1 %collective-permute-start.1 = (bf16[256,128]{1,0:T(8,128)(2,1)S(1)}, bf16[256,128]{1,0:T(8,128)(2,1)}, u32[]{:S(2)}, u32[]{:S(2)}) collective-permute-start(bf16[256,128]{1,0:T(8,128)(2,1)S(1)} %copy.96), channel_id=1, source_target_pairs={{0,8},{8,16},{16,24},{24,32},{32,40},{40,48},{48,56},{56,64},{64,7... | collective-permute-start | bytes 196616 | tf_op jit(solution)/shard_map/while/body/eval_jaxpr/ppermute | solution.py:16
  92.0 11.8 %collective-permute-start = (bf16[256,128]{1,0:T(8,128)(2,1)S(1)}, bf16[256,128]{1,0:T(8,128)(2,1)}, u32[]{:S(2)}, u32[]{:S(2)}) collective-permute-start(bf16[256,128]{1,0:T(8,128)(2,1)S(1)} %copy.95), channel_id=1, source_target_pairs={{0,8},{8,16},{16,24},{24,32},{32,40},{40,48},{48,56},{56,64},{64,7... | collective-permute-start | bytes 196616 | tf_op jit(solution)/shard_map/while/body/eval_jaxpr/ppermute | solution.py:16
  92.8 10.9 %collective-permute-start.1 = (bf16[256,128]{1,0:T(8,128)(2,1)S(1)}, bf16[256,128]{1,0:T(8,128)(2,1)}, u32[]{:S(2)}, u32[]{:S(2)}) collective-permute-start(bf16[256,128]{1,0:T(8,128)(2,1)S(1)} %copy.96), channel_id=1, source_target_pairs={{0,8},{8,16},{16,24},{24,32},{32,40},{40,48},{48,56},{56,64},{64,7... | collective-permute-start | bytes 196616 | tf_op jit(solution)/shard_map/while/body/eval_jaxpr/ppermute | solution.py:16
  107.6 10.9 %collective-permute-start = (bf16[256,128]{1,0:T(8,128)(2,1)S(1)}, bf16[256,128]{1,0:T(8,128)(2,1)}, u32[]{:S(2)}, u32[]{:S(2)}) collective-permute-start(bf16[256,128]{1,0:T(8,128)(2,1)S(1)} %copy.95), channel_id=1, source_target_pairs={{0,8},{8,16},{16,24},{24,32},{32,40},{40,48},{48,56},{56,64},{64,7... | collective-permute-start | bytes 196616 | tf_op jit(solution)/shard_map/while/body/eval_jaxpr/ppermute | solution.py:16
  108.5 10.0 %collective-permute-start.1 = (bf16[256,128]{1,0:T(8,128)(2,1)S(1)}, bf16[256,128]{1,0:T(8,128)(2,1)}, u32[]{:S(2)}, u32[]{:S(2)}) collective-permute-start(bf16[256,128]{1,0:T(8,128)(2,1)S(1)} %copy.96), channel_id=1, source_target_pairs={{0,8},{8,16},{16,24},{24,32},{32,40},{40,48},{48,56},{56,64},{64,7... | collective-permute-start | bytes 196616 | tf_op jit(solution)/shard_map/while/body/eval_jaxpr/ppermute | solution.py:16
  123.3 10.8 %collective-permute-start = (bf16[256,128]{1,0:T(8,128)(2,1)S(1)}, bf16[256,128]{1,0:T(8,128)(2,1)}, u32[]{:S(2)}, u32[]{:S(2)}) collective-permute-start(bf16[256,128]{1,0:T(8,128)(2,1)S(1)} %copy.95), channel_id=1, source_target_pairs={{0,8},{8,16},{16,24},{24,32},{32,40},{40,48},{48,56},{56,64},{64,7... | collective-permute-start | bytes 196616 | tf_op jit(solution)/shard_map/while/body/eval_jaxpr/ppermute | solution.py:16
  138.9 10.8 %collective-permute-start = (bf16[256,128]{1,0:T(8,128)(2,1)S(1)}, bf16[256,128]{1,0:T(8,128)(2,1)}, u32[]{:S(2)}, u32[]{:S(2)}) collective-permute-start(bf16[256,128]{1,0:T(8,128)(2,1)S(1)} %copy.95), channel_id=1, source_target_pairs={{0,8},{8,16},{16,24},{24,32},{32,40},{40,48},{48,56},{56,64},{64,7... | collective-permute-start | bytes 196616 | tf_op jit(solution)/shard_map/while/body/eval_jaxpr/ppermute | solution.py:16
  139.8 10.0 %collective-permute-start.1 = (bf16[256,128]{1,0:T(8,128)(2,1)S(1)}, bf16[256,128]{1,0:T(8,128)(2,1)}, u32[]{:S(2)}, u32[]{:S(2)}) collective-permute-start(bf16[256,128]{1,0:T(8,128)(2,1)S(1)} %copy.96), channel_id=1, source_target_pairs={{0,8},{8,16},{16,24},{24,32},{32,40},{40,48},{48,56},{56,64},{64,7... | collective-permute-start | bytes 196616 | tf_op jit(solution)/shard_map/while/body/eval_jaxpr/ppermute | solution.py:16
  154.6 10.8 %collective-permute-start = (bf16[256,128]{1,0:T(8,128)(2,1)S(1)}, bf16[256,128]{1,0:T(8,128)(2,1)}, u32[]{:S(2)}, u32[]{:S(2)}) collective-permute-start(bf16[256,128]{1,0:T(8,128)(2,1)S(1)} %copy.95), channel_id=1, source_target_pairs={{0,8},{8,16},{16,24},{24,32},{32,40},{40,48},{48,56},{56,64},{64,7... | collective-permute-start | bytes 196616 | tf_op jit(solution)/shard_map/while/body/eval_jaxpr/ppermute | solution.py:16
  170.2 10.8 %collective-permute-start = (bf16[256,128]{1,0:T(8,128)(2,1)S(1)}, bf16[256,128]{1,0:T(8,128)(2,1)}, u32[]{:S(2)}, u32[]{:S(2)}) collective-permute-start(bf16[256,128]{1,0:T(8,128)(2,1)S(1)} %copy.95), channel_id=1, source_target_pairs={{0,8},{8,16},{16,24},{24,32},{32,40},{40,48},{48,56},{56,64},{64,7... | collective-permute-start | bytes 196616 | tf_op jit(solution)/shard_map/while/body/eval_jaxpr/ppermute | solution.py:16
  171.1 10.0 %collective-permute-start.1 = (bf16[256,128]{1,0:T(8,128)(2,1)S(1)}, bf16[256,128]{1,0:T(8,128)(2,1)}, u32[]{:S(2)}, u32[]{:S(2)}) collective-permute-start(bf16[256,128]{1,0:T(8,128)(2,1)S(1)} %copy.96), channel_id=1, source_target_pairs={{0,8},{8,16},{16,24},{24,32},{32,40},{40,48},{48,56},{56,64},{64,7... | collective-permute-start | bytes 196616 | tf_op jit(solution)/shard_map/while/body/eval_jaxpr/ppermute | solution.py:16
  185.9 10.8 %collective-permute-start = (bf16[256,128]{1,0:T(8,128)(2,1)S(1)}, bf16[256,128]{1,0:T(8,128)(2,1)}, u32[]{:S(2)}, u32[]{:S(2)}) collective-permute-start(bf16[256,128]{1,0:T(8,128)(2,1)S(1)} %copy.95), channel_id=1, source_target_pairs={{0,8},{8,16},{16,24},{24,32},{32,40},{40,48},{48,56},{56,64},{64,7... | collective-permute-start | bytes 196616 | tf_op jit(solution)/shard_map/while/body/eval_jaxpr/ppermute | solution.py:16
  201.6 10.8 %collective-permute-start = (bf16[256,128]{1,0:T(8,128)(2,1)S(1)}, bf16[256,128]{1,0:T(8,128)(2,1)}, u32[]{:S(2)}, u32[]{:S(2)}) collective-permute-start(bf16[256,128]{1,0:T(8,128)(2,1)S(1)} %copy.95), channel_id=1, source_target_pairs={{0,8},{8,16},{16,24},{24,32},{32,40},{40,48},{48,56},{56,64},{64,7... | collective-permute-start | bytes 196616 | tf_op jit(solution)/shard_map/while/body/eval_jaxpr/ppermute | solution.py:16
  202.4 10.0 %collective-permute-start.1 = (bf16[256,128]{1,0:T(8,128)(2,1)S(1)}, bf16[256,128]{1,0:T(8,128)(2,1)}, u32[]{:S(2)}, u32[]{:S(2)}) collective-permute-start(bf16[256,128]{1,0:T(8,128)(2,1)S(1)} %copy.96), channel_id=1, source_target_pairs={{0,8},{8,16},{16,24},{24,32},{32,40},{40,48},{48,56},{56,64},{64,7... | collective-permute-start | bytes 196616 | tf_op jit(solution)/shard_map/while/body/eval_jaxpr/ppermute | solution.py:16
  217.2 10.8 %collective-permute-start = (bf16[256,128]{1,0:T(8,128)(2,1)S(1)}, bf16[256,128]{1,0:T(8,128)(2,1)}, u32[]{:S(2)}, u32[]{:S(2)}) collective-permute-start(bf16[256,128]{1,0:T(8,128)(2,1)S(1)} %copy.95), channel_id=1, source_target_pairs={{0,8},{8,16},{16,24},{24,32},{32,40},{40,48},{48,56},{56,64},{64,7... | collective-permute-start | bytes 196616 | tf_op jit(solution)/shard_map/while/body/eval_jaxpr/ppermute | solution.py:16
  232.9 10.8 %collective-permute-start = (bf16[256,128]{1,0:T(8,128)(2,1)S(1)}, bf16[256,128]{1,0:T(8,128)(2,1)}, u32[]{:S(2)}, u32[]{:S(2)}) collective-permute-start(bf16[256,128]{1,0:T(8,128)(2,1)S(1)} %copy.95), channel_id=1, source_target_pairs={{0,8},{8,16},{16,24},{24,32},{32,40},{40,48},{48,56},{56,64},{64,7... | collective-permute-start | bytes 196616 | tf_op jit(solution)/shard_map/while/body/eval_jaxpr/ppermute | solution.py:16
  233.7 10.0 %collective-permute-start.1 = (bf16[256,128]{1,0:T(8,128)(2,1)S(1)}, bf16[256,128]{1,0:T(8,128)(2,1)}, u32[]{:S(2)}, u32[]{:S(2)}) collective-permute-start(bf16[256,128]{1,0:T(8,128)(2,1)S(1)} %copy.96), channel_id=1, source_target_pairs={{0,8},{8,16},{16,24},{24,32},{32,40},{40,48},{48,56},{56,64},{64,7... | collective-permute-start | bytes 196616 | tf_op jit(solution)/shard_map/while/body/eval_jaxpr/ppermute | solution.py:16
  248.5 10.8 %collective-permute-start = (bf16[256,128]{1,0:T(8,128)(2,1)S(1)}, bf16[256,128]{1,0:T(8,128)(2,1)}, u32[]{:S(2)}, u32[]{:S(2)}) collective-permute-start(bf16[256,128]{1,0:T(8,128)(2,1)S(1)} %copy.95), channel_id=1, source_target_pairs={{0,8},{8,16},{16,24},{24,32},{32,40},{40,48},{48,56},{56,64},{64,7... | collective-permute-start | bytes 196616 | tf_op jit(solution)/shard_map/while/body/eval_jaxpr/ppermute | solution.py:16
  264.2 10.8 %collective-permute-start = (bf16[256,128]{1,0:T(8,128)(2,1)S(1)}, bf16[256,128]{1,0:T(8,128)(2,1)}, u32[]{:S(2)}, u32[]{:S(2)}) collective-permute-start(bf16[256,128]{1,0:T(8,128)(2,1)S(1)} %copy.95), channel_id=1, source_target_pairs={{0,8},{8,16},{16,24},{24,32},{32,40},{40,48},{48,56},{56,64},{64,7... | collective-permute-start | bytes 196616 | tf_op jit(solution)/shard_map/while/body/eval_jaxpr/ppermute | solution.py:16
  265.0 10.0 %collective-permute-start.1 = (bf16[256,128]{1,0:T(8,128)(2,1)S(1)}, bf16[256,128]{1,0:T(8,128)(2,1)}, u32[]{:S(2)}, u32[]{:S(2)}) collective-permute-start(bf16[256,128]{1,0:T(8,128)(2,1)S(1)} %copy.96), channel_id=1, source_target_pairs={{0,8},{8,16},{16,24},{24,32},{32,40},{40,48},{48,56},{56,64},{64,7... | collective-permute-start | bytes 196616 | tf_op jit(solution)/shard_map/while/body/eval_jaxpr/ppermute | solution.py:16
  279.9 10.8 %collective-permute-start = (bf16[256,128]{1,0:T(8,128)(2,1)S(1)}, bf16[256,128]{1,0:T(8,128)(2,1)}, u32[]{:S(2)}, u32[]{:S(2)}) collective-permute-start(bf16[256,128]{1,0:T(8,128)(2,1)S(1)} %copy.95), channel_id=1, source_target_pairs={{0,8},{8,16},{16,24},{24,32},{32,40},{40,48},{48,56},{56,64},{64,7... | collective-permute-start | bytes 196616 | tf_op jit(solution)/shard_map/while/body/eval_jaxpr/ppermute | solution.py:16
  295.5 10.8 %collective-permute-start = (bf16[256,128]{1,0:T(8,128)(2,1)S(1)}, bf16[256,128]{1,0:T(8,128)(2,1)}, u32[]{:S(2)}, u32[]{:S(2)}) collective-permute-start(bf16[256,128]{1,0:T(8,128)(2,1)S(1)} %copy.95), channel_id=1, source_target_pairs={{0,8},{8,16},{16,24},{24,32},{32,40},{40,48},{48,56},{56,64},{64,7... | collective-permute-start | bytes 196616 | tf_op jit(solution)/shard_map/while/body/eval_jaxpr/ppermute | solution.py:16
  296.4 10.0 %collective-permute-start.1 = (bf16[256,128]{1,0:T(8,128)(2,1)S(1)}, bf16[256,128]{1,0:T(8,128)(2,1)}, u32[]{:S(2)}, u32[]{:S(2)}) collective-permute-start(bf16[256,128]{1,0:T(8,128)(2,1)S(1)} %copy.96), channel_id=1, source_target_pairs={{0,8},{8,16},{16,24},{24,32},{32,40},{40,48},{48,56},{56,64},{64,7... | collective-permute-start | bytes 196616 | tf_op jit(solution)/shard_map/while/body/eval_jaxpr/ppermute | solution.py:16
  311.2 10.8 %collective-permute-start = (bf16[256,128]{1,0:T(8,128)(2,1)S(1)}, bf16[256,128]{1,0:T(8,128)(2,1)}, u32[]{:S(2)}, u32[]{:S(2)}) collective-permute-start(bf16[256,128]{1,0:T(8,128)(2,1)S(1)} %copy.95), channel_id=1, source_target_pairs={{0,8},{8,16},{16,24},{24,32},{32,40},{40,48},{48,56},{56,64},{64,7... | collective-permute-start | bytes 196616 | tf_op jit(solution)/shard_map/while/body/eval_jaxpr/ppermute | solution.py:16
  326.8 10.8 %collective-permute-start = (bf16[256,128]{1,0:T(8,128)(2,1)S(1)}, bf16[256,128]{1,0:T(8,128)(2,1)}, u32[]{:S(2)}, u32[]{:S(2)}) collective-permute-start(bf16[256,128]{1,0:T(8,128)(2,1)S(1)} %copy.95), channel_id=1, source_target_pairs={{0,8},{8,16},{16,24},{24,32},{32,40},{40,48},{48,56},{56,64},{64,7... | collective-permute-start | bytes 196616 | tf_op jit(solution)/shard_map/while/body/eval_jaxpr/ppermute | solution.py:16
  327.7 10.0 %collective-permute-start.1 = (bf16[256,128]{1,0:T(8,128)(2,1)S(1)}, bf16[256,128]{1,0:T(8,128)(2,1)}, u32[]{:S(2)}, u32[]{:S(2)}) collective-permute-start(bf16[256,128]{1,0:T(8,128)(2,1)S(1)} %copy.96), channel_id=1, source_target_pairs={{0,8},{8,16},{16,24},{24,32},{32,40},{40,48},{48,56},{56,64},{64,7... | collective-permute-start | bytes 196616 | tf_op jit(solution)/shard_map/while/body/eval_jaxpr/ppermute | solution.py:16
  342.5 10.8 %collective-permute-start = (bf16[256,128]{1,0:T(8,128)(2,1)S(1)}, bf16[256,128]{1,0:T(8,128)(2,1)}, u32[]{:S(2)}, u32[]{:S(2)}) collective-permute-start(bf16[256,128]{1,0:T(8,128)(2,1)S(1)} %copy.95), channel_id=1, source_target_pairs={{0,8},{8,16},{16,24},{24,32},{32,40},{40,48},{48,56},{56,64},{64,7... | collective-permute-start | bytes 196616 | tf_op jit(solution)/shard_map/while/body/eval_jaxpr/ppermute | solution.py:16
  358.2 10.8 %collective-permute-start = (bf16[256,128]{1,0:T(8,128)(2,1)S(1)}, bf16[256,128]{1,0:T(8,128)(2,1)}, u32[]{:S(2)}, u32[]{:S(2)}) collective-permute-start(bf16[256,128]{1,0:T(8,128)(2,1)S(1)} %copy.95), channel_id=1, source_target_pairs={{0,8},{8,16},{16,24},{24,32},{32,40},{40,48},{48,56},{56,64},{64,7... | collective-permute-start | bytes 196616 | tf_op jit(solution)/shard_map/while/body/eval_jaxpr/ppermute | solution.py:16
  359.0 10.0 %collective-permute-start.1 = (bf16[256,128]{1,0:T(8,128)(2,1)S(1)}, bf16[256,128]{1,0:T(8,128)(2,1)}, u32[]{:S(2)}, u32[]{:S(2)}) collective-permute-start(bf16[256,128]{1,0:T(8,128)(2,1)S(1)} %copy.96), channel_id=1, source_target_pairs={{0,8},{8,16},{16,24},{24,32},{32,40},{40,48},{48,56},{56,64},{64,7... | collective-permute-start | bytes 196616 | tf_op jit(solution)/shard_map/while/body/eval_jaxpr/ppermute | solution.py:16
  373.8 10.8 %collective-permute-start = (bf16[256,128]{1,0:T(8,128)(2,1)S(1)}, bf16[256,128]{1,0:T(8,128)(2,1)}, u32[]{:S(2)}, u32[]{:S(2)}) collective-permute-start(bf16[256,128]{1,0:T(8,128)(2,1)S(1)} %copy.95), channel_id=1, source_target_pairs={{0,8},{8,16},{16,24},{24,32},{32,40},{40,48},{48,56},{56,64},{64,7... | collective-permute-start | bytes 196616 | tf_op jit(solution)/shard_map/while/body/eval_jaxpr/ppermute | solution.py:16
  389.5 10.8 %collective-permute-start = (bf16[256,128]{1,0:T(8,128)(2,1)S(1)}, bf16[256,128]{1,0:T(8,128)(2,1)}, u32[]{:S(2)}, u32[]{:S(2)}) collective-permute-start(bf16[256,128]{1,0:T(8,128)(2,1)S(1)} %copy.95), channel_id=1, source_target_pairs={{0,8},{8,16},{16,24},{24,32},{32,40},{40,48},{48,56},{56,64},{64,7... | collective-permute-start | bytes 196616 | tf_op jit(solution)/shard_map/while/body/eval_jaxpr/ppermute | solution.py:16
  405.1 10.8 %collective-permute-start = (bf16[256,128]{1,0:T(8,128)(2,1)S(1)}, bf16[256,128]{1,0:T(8,128)(2,1)}, u32[]{:S(2)}, u32[]{:S(2)}) collective-permute-start(bf16[256,128]{1,0:T(8,128)(2,1)S(1)} %copy.95), channel_id=1, source_target_pairs={{0,8},{8,16},{16,24},{24,32},{32,40},{40,48},{48,56},{56,64},{64,7... | collective-permute-start | bytes 196616 | tf_op jit(solution)/shard_map/while/body/eval_jaxpr/ppermute | solution.py:16
  420.8 10.8 %collective-permute-start = (bf16[256,128]{1,0:T(8,128)(2,1)S(1)}, bf16[256,128]{1,0:T(8,128)(2,1)}, u32[]{:S(2)}, u32[]{:S(2)}) collective-permute-start(bf16[256,128]{1,0:T(8,128)(2,1)S(1)} %copy.95), channel_id=1, source_target_pairs={{0,8},{8,16},{16,24},{24,32},{32,40},{40,48},{48,56},{56,64},{64,7... | collective-permute-start | bytes 196616 | tf_op jit(solution)/shard_map/while/body/eval_jaxpr/ppermute | solution.py:16
  421.6 10.0 %collective-permute-start.1 = (bf16[256,128]{1,0:T(8,128)(2,1)S(1)}, bf16[256,128]{1,0:T(8,128)(2,1)}, u32[]{:S(2)}, u32[]{:S(2)}) collective-permute-start(bf16[256,128]{1,0:T(8,128)(2,1)S(1)} %copy.96), channel_id=1, source_target_pairs={{0,8},{8,16},{16,24},{24,32},{32,40},{40,48},{48,56},{56,64},{64,7... | collective-permute-start | bytes 196616 | tf_op jit(solution)/shard_map/while/body/eval_jaxpr/ppermute | solution.py:16
  436.5 10.8 %collective-permute-start = (bf16[256,128]{1,0:T(8,128)(2,1)S(1)}, bf16[256,128]{1,0:T(8,128)(2,1)}, u32[]{:S(2)}, u32[]{:S(2)}) collective-permute-start(bf16[256,128]{1,0:T(8,128)(2,1)S(1)} %copy.95), channel_id=1, source_target_pairs={{0,8},{8,16},{16,24},{24,32},{32,40},{40,48},{48,56},{56,64},{64,7... | collective-permute-start | bytes 196616 | tf_op jit(solution)/shard_map/while/body/eval_jaxpr/ppermute | solution.py:16
  452.1 10.8 %collective-permute-start = (bf16[256,128]{1,0:T(8,128)(2,1)S(1)}, bf16[256,128]{1,0:T(8,128)(2,1)}, u32[]{:S(2)}, u32[]{:S(2)}) collective-permute-start(bf16[256,128]{1,0:T(8,128)(2,1)S(1)} %copy.95), channel_id=1, source_target_pairs={{0,8},{8,16},{16,24},{24,32},{32,40},{40,48},{48,56},{56,64},{64,7... | collective-permute-start | bytes 196616 | tf_op jit(solution)/shard_map/while/body/eval_jaxpr/ppermute | solution.py:16
  467.8 10.8 %collective-permute-start = (bf16[256,128]{1,0:T(8,128)(2,1)S(1)}, bf16[256,128]{1,0:T(8,128)(2,1)}, u32[]{:S(2)}, u32[]{:S(2)}) collective-permute-start(bf16[256,128]{1,0:T(8,128)(2,1)S(1)} %copy.95), channel_id=1, source_target_pairs={{0,8},{8,16},{16,24},{24,32},{32,40},{40,48},{48,56},{56,64},{64,7... | collective-permute-start | bytes 196616 | tf_op jit(solution)/shard_map/while/body/eval_jaxpr/ppermute | solution.py:16
  483.4 10.8 %collective-permute-start = (bf16[256,128]{1,0:T(8,128)(2,1)S(1)}, bf16[256,128]{1,0:T(8,128)(2,1)}, u32[]{:S(2)}, u32[]{:S(2)}) collective-permute-start(bf16[256,128]{1,0:T(8,128)(2,1)S(1)} %copy.95), channel_id=1, source_target_pairs={{0,8},{8,16},{16,24},{24,32},{32,40},{40,48},{48,56},{56,64},{64,7... | collective-permute-start | bytes 196616 | tf_op jit(solution)/shard_map/while/body/eval_jaxpr/ppermute | solution.py:16
  499.1 10.8 %collective-permute-start = (bf16[256,128]{1,0:T(8,128)(2,1)S(1)}, bf16[256,128]{1,0:T(8,128)(2,1)}, u32[]{:S(2)}, u32[]{:S(2)}) collective-permute-start(bf16[256,128]{1,0:T(8,128)(2,1)S(1)} %copy.95), channel_id=1, source_target_pairs={{0,8},{8,16},{16,24},{24,32},{32,40},{40,48},{48,56},{56,64},{64,7... | collective-permute-start | bytes 196616 | tf_op jit(solution)/shard_map/while/body/eval_jaxpr/ppermute | solution.py:16
  530.9 204.2 %reduce-scatter.7.cloned.1.call-start = ((), (), s32[]{:S(2)}) async-start(), calls=%async_computation.2 | async-start | bytes 5406720
  (150 other events, 1277.5 us)
Sparse Core Ops, SparseCore 0:
  531.0 78.7 reduce-scatter.8
  612.3 122.7 reduce-scatter.6
where the time goes:
time: 753 us; the launch traced here: 745 us
  waiting for transfers between devices  307 us (41%)
  matrix products  237 us (31%)
  local copies, waits for them, and re-layouts  122 us (16%)
  loops' own time  42.2 us (6%)
  between operations  16.9 us (2%)
  starting transfers between devices  14.5 us (2%)
    unnamed x4, waiting for transfers between devices  188 us
    ppermute x126, waiting for transfers between devices, shifted(): return lax.ppermute(value, axis, pairs)  119 us
    dot_general x32, matrix products, tile_grads(): jnp.einsum('hgqk,khd->qhgd', dscores_low, key_tile, preferred_element_typ...  94.5 us
    while x186, local copies, waits for them, and re-layouts  69.8 us
    dot_general x32, matrix products, tile_grads(): jnp.einsum('qhgd,khd->hgqk', q_tile, key_tile, preferred_element_type=jnp...  51.9 us
    another operation x1, loops' own time, shards(): lax.fori_loop(0, cycle_size - 1, cycle_step, (dq_start, key_act, value_ac...  42.2 us
    dot_general x32, matrix products, tile_grads(): jnp.einsum('hgqk,qhgd->khd', probs_low, grad_tile, preferred_element_type...  34.4 us
    dot_general x32, matrix products, tile_grads(): jnp.einsum('hgqk,qhgd->khd', dscores_low, q_tile, preferred_element_type=...  34 us
  transfers between devices with their start and end apart: 128, of which 65 were waited for; matrix products, arithmetic and copies ran while one was open for 39% of the time, Pallas kernels for 0%

commit v1 on v0

v1 whole, which is shorter than its diff:
```python
import functools
import math

import jax
import jax.numpy as jnp
from jax import lax
from jax.experimental import pallas as pl
from jax.experimental.pallas import tpu as pltpu
from jax.sharding import PartitionSpec as P

BF = jnp.bfloat16
F32 = jnp.float32
MESH = pl.DeviceIdType.MESH
SCALE = 1.0 / math.sqrt(128)
LOG2E = math.log2(math.e)
NT = (((1,), (1,)), ((), ()))
TN = (((0,), (0,)), ((), ()))
SPAN = 128
TP = 8
NZ = 8
FEAT = 640
HALF_FEAT = 320
WROWS = 160

dot = functools.partial(lax.dot_general, preferred_element_type=F32)


def mm(a, b):
    return jnp.dot(a, b, preferred_element_type=F32)


def place():
    i = lax.axis_index("ctx")
    core = i % 2
    z = (i // 2) % NZ
    y = i // 16
    rank = jnp.where(core == 0, z, 7 - z)
    return i, core, z, y, rank


def ctx_of(y, z, core):
    return y * 16 + z * 2 + core


def remote(src, dst, send, recv, **where):
    return pltpu.make_async_remote_copy(
        src_ref=src, dst_ref=dst, send_sem=send, recv_sem=recv, device_id=where, device_id_type=MESH
    )


def neighbours(core, z, y):
    up = (z + 1) % NZ
    down = (z + NZ - 1) % NZ
    nxt = ctx_of(y, jnp.where(core == 0, up, down), core)
    prv = ctx_of(y, jnp.where(core == 0, down, up), core)
    return nxt, prv, ctx_of(1 - y, z, core), ctx_of(y, z, 1 - core)


def attention_kernel(
    swapped, q_in, k_in, v_in, o_in, d_in, ln_in, wk, wv,
    dq_out, dk_out, dv_out, wbuf,
    qb, db, ob, lnc, lnb, deb, dqa, kv, acc, sin, sout, dqs, dqr, ys, yr,
    xsend, xrecv, zsend, zrecv, ysend, yrecv, ssend, srecv, wsend, wrecv, fsend, frecv, dsem, lsem,
):
    i, core, z, y, rank = place()
    tp = lax.axis_index("tp")
    other = 1 - core
    nxt, prv, ypart, mate = neighbours(core, z, y)
    odd = rank % 2
    pair = rank // 2
    chip = y * NZ + z

    barrier = pltpu.get_barrier_semaphore()
    for dev in (nxt, prv, ypart, mate):
        pl.semaphore_signal(barrier, inc=1, device_id={"ctx": dev}, device_id_type=MESH)
    for step in range(1, TP):
        pl.semaphore_signal(
            barrier, inc=1, device_id={"tp": (tp + step) % TP}, device_id_type=MESH
        )

    flip_wide = jnp.concatenate([swapped[...]] * 16, axis=0)
    flip16 = flip_wide.astype(BF) > 0.5

    def canon(first, second, hl):
        return jnp.where(flip16, second, first) if hl == 0 else jnp.where(flip16, first, second)

    for hl in range(2):
        kv[y, rank, hl] = canon(k_in[:SPAN, :], k_in[SPAN:, :], hl)
        kv[y, rank, 2 + hl] = canon(v_in[:SPAN, :], v_in[SPAN:, :], hl)
    pl.semaphore_wait(barrier, 4 + TP - 1)

    def gather_z(s):
        block = kv.at[y, (rank - s + NZ) % NZ]
        return remote(block, block, zsend.at[s], zrecv.at[s + 1], ctx=nxt)

    def gather_y(s):
        block = kv.at[y, (rank - s + NZ) % NZ]
        return remote(block, block, ysend.at[s], yrecv.at[s], ctx=ypart)

    gather_z(0).start()
    gather_y(0).start()

    for hl in range(2):
        for h in range(8):
            cols = slice(h * 128, (h + 1) * 128)
            for full, here in ((qb, q_in), (db, d_in), (ob, o_in)):
                full[core, hl, cols, :] = canon(here[:SPAN, cols], here[SPAN:, cols], hl)
    both = ln_in[...] * LOG2E
    flip8 = swapped[...] > 0.5
    lnc[core, 0] = jnp.where(flip8, both[:, SPAN:], both[:, :SPAN])
    lnc[core, 1] = jnp.where(flip8, both[:, :SPAN], both[:, SPAN:])
    swaps = [
        remote(ref.at[core], ref.at[core], xsend.at[n], xrecv.at[n], ctx=mate)
        for n, ref in enumerate((qb, db, ob, lnc))
    ]
    for swap in swaps:
        swap.start()

    def zero(n, _):
        for part in range(4):
            acc[n // NZ, n % NZ, part] = jnp.zeros((128, 128), F32)
        return 0

    lax.fori_loop(0, 2 * NZ, zero, 0)
    dqa[...] = jnp.zeros_like(dqa)

    ones = jnp.ones((128, 128), BF)
    head_of = lax.broadcasted_iota(jnp.int32, (32, 1024), 1) // 128
    pick = (lax.broadcasted_iota(jnp.int32, (32, 1024), 0) % 8 == head_of).astype(F32).astype(BF)

    def row_terms(slot):
        for hl in range(2):
            prod = db[slot, hl].astype(F32) * ob[slot, hl].astype(F32)
            high = prod.astype(BF)
            low = (prod - high.astype(F32)).astype(BF)
            deb[slot, hl] = mm(high, ones) + mm(low, ones)
            norm = lnc[slot, hl]
            p1 = norm.astype(BF)
            rest = norm - p1.astype(F32)
            p2 = rest.astype(BF)
            rest = rest - p2.astype(F32)
            p3 = rest.astype(BF)
            parts = jnp.concatenate(
                [p1.astype(F32), p2.astype(F32), p3.astype(F32), jnp.zeros((8, 128), F32)], axis=0
            ).astype(BF)
            wide = dot(parts, pick, TN)
            for h in range(8):
                lnb[slot, hl, h * 128 : (h + 1) * 128, :] = wide[:, h * 128 : (h + 1) * 128]

    row_terms(core)
    for swap in swaps:
        swap.wait()
    row_terms(other)

    def pump(s):
        remote(
            kv.at[y, (rank - s + NZ) % NZ], kv.at[y, (rank - s + NZ) % NZ],
            zsend.at[0], zrecv.at[s], ctx=nxt,
        ).wait_recv()
        gather_y(s).start()

        @pl.when(s < NZ - 1)
        def _():
            gather_z(s).start()

    pump(1)
    pump(2)

    def z_of(rk):
        return jnp.where(core == 0, rk, 7 - rk)

    def unit(yp, w, hk, hq, masked):
        ra = 2 * w
        rb = 2 * w + 1
        k = jnp.concatenate([kv[yp, ra, hk], kv[yp, rb, hk]], axis=0)
        v = jnp.concatenate([kv[yp, ra, 2 + hk], kv[yp, rb, 2 + hk]], axis=0)
        gk = None
        gv = None
        for slot in range(2):
            q = qb[slot, hq]
            d = db[slot, hq]
            ln = lnb[slot, hq]
            de = deb[slot, hq]
            scores = dot(q, k, NT)
            dp = dot(d, v, NT)
            prob = jnp.exp2(scores * (SCALE * LOG2E) - jnp.concatenate([ln, ln], axis=1))
            if masked:
                qi = 2 * chip + slot
                qspan = jnp.where(hq == 0, qi, 63 - qi)
                shape = (1024, 128)
                gap = (
                    lax.broadcasted_iota(jnp.int32, shape, 0) % SPAN
                    - lax.broadcasted_iota(jnp.int32, shape, 1)
                )
                seen = []
                for rk in (ra, rb):
                    ki = 2 * (yp * NZ + z_of(rk)) + core
                    kspan = jnp.where(hk == 0, ki, 63 - ki)
                    seen.append(gap >= (kspan - qspan) * SPAN)
                prob = jnp.concatenate(
                    [
                        jnp.where(seen[0], prob[:, :128], 0.0),
                        jnp.where(seen[1], prob[:, 128:], 0.0),
                    ],
                    axis=1,
                )
            ds = (prob * (dp - jnp.concatenate([de, de], axis=1))).astype(BF)
            pr = prob.astype(BF)
            dqa[slot, hq] += mm(ds, k)
            gk = dot(q, ds, TN) if gk is None else gk + dot(q, ds, TN)
            gv = dot(d, pr, TN) if gv is None else gv + dot(d, pr, TN)
        acc[yp, ra, hk] += gk[:, :128]
        acc[yp, rb, hk] += gk[:, 128:]
        acc[yp, ra, 2 + hk] += gv[:, :128]
        acc[yp, rb, 2 + hk] += gv[:, 128:]

    def where_at(x):
        n = x // 2
        w = (pair - n - (1 - odd) + 8) % 4
        yp = (y + x) % 2
        return w, yp

    def sum_copy(yp, rk):
        return remote(sout.at[yp, rk], sin.at[yp, rk], ssend.at[yp, rk], srecv.at[yp, rk], ctx=nxt)

    def pass_sums(x):
        w, yp = where_at(x)
        for rk in (2 * w + 1, 2 * w):
            s = (rank - rk + NZ) % NZ

            @pl.when(s == 1)
            def _():
                sout[yp, rk] = acc[yp, rk].astype(BF)

            @pl.when(s > 1)
            def _():
                sum_copy(yp, rk).wait_recv()
                sout[yp, rk] = (acc[yp, rk] + sin[yp, rk].astype(F32)).astype(BF)

            @pl.when(s > 0)
            def _():
                sum_copy(yp, rk).start()

    def weight_copies(step):
        peer = (tp + step) % TP
        out = []
        for n, ref in enumerate((wk, wv)):
            rows = pl.ds(pl.multiple_of(peer * FEAT + core * HALF_FEAT, 64), HALF_FEAT)
            mine = pl.ds(pl.multiple_of(core * HALF_FEAT, 64), HALF_FEAT)
            out.append(
                remote(
                    ref.at[rows, :], wbuf.at[tp, n, mine, :],
                    wsend.at[step, n], wrecv.at[step, n], tp=peer,
                )
            )
        return out

    def weight_forwards(step):
        giver = (tp + TP - step) % TP
        out = []
        for n in range(2):
            mine = pl.ds(pl.multiple_of(core * HALF_FEAT, 64), HALF_FEAT)
            block = wbuf.at[giver, n, mine, :]
            out.append(remote(block, block, fsend.at[step, n], frecv.at[step, n], ctx=mate))
        return out

    def half_step(x, _):
        w, yp = where_at(x)
        g = x % 2

        @pl.when(g == 1)
        def _():
            for rk in (2 * w + 1, 2 * w):
                s = (rank - rk + NZ) % NZ
                block = kv.at[yp, rk]
                remote(block, block, ysend.at[0], yrecv.at[s], ctx=ypart).wait_recv()

        @pl.when(x > 0)
        def _():
            for copy in weight_copies(x):
                copy.start()

        unit(yp, w, 0, 1, False)
        own = jnp.logical_and(g == 0, w == pair)

        @pl.when(own)
        def _():
            def masked_unit(hl, _):
                unit(yp, w, hl, hl, True)
                return 0

            lax.fori_loop(0, 2, masked_unit, 0)

        @pl.when(jnp.logical_not(own))
        def _():
            hl = jnp.where(yp * NZ + z_of(2 * w) < chip, 0, 1)
            unit(yp, w, hl, hl, False)

        @pl.when(x < 5)
        def _():
            pump(x + 3)

        @pl.when(x > 1)
        def _():
            for copy in weight_copies(x - 1):
                copy.wait_recv()
            for copy in weight_forwards(x - 1):
                copy.start()

        ready = x - (1 - odd)

        @pl.when(ready >= 0)
        def _():
            pass_sums(ready)

        return 0

    lax.fori_loop(0, 8, half_step, 0)

    dqs[...] = (dqa[other] * SCALE).astype(BF)
    dq_copy = remote(dqs, dqr, dsem.at[0], dsem.at[1], ctx=mate)
    dq_copy.start()

    @pl.when(odd == 0)
    def _():
        pass_sums(7)

    for copy in weight_copies(TP - 1):
        copy.wait_recv()
    for copy in weight_forwards(TP - 1):
        copy.start()

    sum_copy(1 - y, rank).wait_recv()
    ys[...] = (acc[1 - y, rank] + sin[1 - y, rank].astype(F32)).astype(BF)
    y_copy = remote(ys, yr, dsem.at[2], dsem.at[3], ctx=ypart)
    y_copy.start()

    dq_copy.wait()
    for h in range(8):
        cols = slice(h * 128, (h + 1) * 128)
        low = (dqa[core, 0, cols, :] * SCALE + dqr[0, cols, :].astype(F32)).astype(BF)
        high = (dqa[core, 1, cols, :] * SCALE + dqr[1, cols, :].astype(F32)).astype(BF)
        dq_out[0:SPAN, cols] = jnp.where(flip16, high, low)
        dq_out[SPAN:, cols] = jnp.where(flip16, low, high)

    sum_copy(y, rank).wait_recv()
    y_copy.wait()
    total = acc[y, rank] + sin[y, rank].astype(F32) + yr[...].astype(F32)
    for out, at, factor in ((dk_out, 0, SCALE), (dv_out, 2, 1.0)):
        low = (total[at] * factor).T.astype(BF)
        high = (total[at + 1] * factor).T.astype(BF)
        out[0:SPAN, :] = jnp.where(flip16, high, low)
        out[SPAN:, :] = jnp.where(flip16, low, high)

    def drain(s, _):
        gather_y(s).wait_send()

        @pl.when(s < NZ - 1)
        def _():
            gather_z(s).wait_send()

        @pl.when(s > 0)
        def _():
            for copy in weight_copies(s):
                copy.wait_send()
            for copy in weight_forwards(s):
                copy.wait()
            for yp in range(2):
                sum_copy(yp, (rank - s + NZ) % NZ).wait_send()

        return 0

    lax.fori_loop(0, NZ, drain, 0)


def attention(swapped, q, k, v, o, d, ln, wk, wv):
    vmem = pl.BlockSpec(memory_space=pltpu.VMEM)
    anyw = pl.BlockSpec(memory_space=pl.ANY)
    dma = pltpu.SemaphoreType.DMA
    sds = jax.ShapeDtypeStruct
    rows = (2, 2, 1024, 128)
    block = (4, 128, 128)
    return pl.pallas_call(
        attention_kernel,
        out_shape=[
            sds((256, 1024), BF),
            sds((256, 128), BF),
            sds((256, 128), BF),
            sds((TP, 2, FEAT, 128), BF),
        ],
        in_specs=[vmem] * 7 + [anyw] * 2,
        out_specs=[vmem, vmem, vmem, anyw],
        scratch_shapes=[
            pltpu.VMEM(rows, BF),
            pltpu.VMEM(rows, BF),
            pltpu.VMEM(rows, BF),
            pltpu.VMEM((2, 2, 8, 128), F32),
            pltpu.VMEM(rows, F32),
            pltpu.VMEM(rows, F32),
            pltpu.VMEM(rows, F32),
            pltpu.VMEM((2, NZ) + block, BF),
            pltpu.VMEM((2, NZ) + block, F32),
            pltpu.VMEM((2, NZ) + block, BF),
            pltpu.VMEM((2, NZ) + block, BF),
            pltpu.VMEM((2, 1024, 128), BF),
            pltpu.VMEM((2, 1024, 128), BF),
            pltpu.VMEM(block, BF),
            pltpu.VMEM(block, BF),
            dma((4,)),
            dma((4,)),
            dma((NZ,)),
            dma((NZ,)),
            dma((NZ,)),
            dma((NZ,)),
            dma((2, NZ)),
            dma((2, NZ)),
            dma((TP, 2)),
            dma((TP, 2)),
            dma((TP, 2)),
            dma((TP, 2)),
            dma((4,)),
            dma((1,)),
        ],
        compiler_params=pltpu.CompilerParams(
            collective_id=0, has_side_effects=True, vmem_limit_bytes=48 * 2**20
        ),
        cost_estimate=pl.CostEstimate(
            flops=11 * 10**9, bytes_accessed=10**7, transcendentals=9 * 10**6
        ),
    )(swapped, q, k, v, o, d, ln, wk, wv)


def project_kernel(
    dk, dv, hid, wbuf, wko, wvo,
    gk_out, gv_out, dh_out,
    dkv, gathered, part, cs, cr, rin, rout, ys, yr,
    gsend, grecv, csem, rsend, rrecv, ysem,
):
    i, core, z, y, rank = place()
    tp = lax.axis_index("tp")
    other = 1 - core
    nxt, prv, ypart, mate = neighbours(core, z, y)

    barrier = pltpu.get_barrier_semaphore()
    for dev in (nxt, prv, ypart, mate):
        pl.semaphore_signal(barrier, inc=1, device_id={"ctx": dev}, device_id_type=MESH)
    for step in range(1, TP):
        pl.semaphore_signal(
            barrier, inc=1, device_id={"tp": (tp + step) % TP}, device_id_type=MESH
        )
    dkv[:, 0:128] = dk[...]
    dkv[:, 128:256] = dv[...]
    pl.semaphore_wait(barrier, 4 + TP - 1)

    def spread(step):
        return remote(
            dkv, gathered.at[tp], gsend.at[step], grecv.at[step], tp=(tp + step) % TP
        )

    for step in range(1, TP):
        spread(step).start()

    mine = dkv[...]
    for n in range(8):
        part[pl.ds(n * 640, 640), :] = dot(hid[:, n * 640 : (n + 1) * 640], mine, TN)

    def rows_of(c, k):
        return pl.ds(pl.multiple_of((c * 2 + k) * WROWS, 32), WROWS)

    def fill(c, _):
        cs[c] = part[rows_of(c, other), :].astype(BF)
        return 0

    lax.fori_loop(0, 16, fill, 0)
    swap = remote(cs, cr, csem.at[0], csem.at[1], ctx=mate)
    swap.start()

    total = mm(mine[:, :128], wko[...].T) + mm(mine[:, 128:], wvo[...].T)
    dh_out[...] = total.astype(BF)
    swap.wait()

    def z_of(rk):
        return jnp.where(core == 0, rk, 7 - rk)

    def own_part(yp, rk):
        c = yp * NZ + z_of(rk)
        return part[rows_of(c, core), :] + cr[c].astype(F32)

    def chain(yp, s):
        rk = (rank - s + NZ) % NZ
        return remote(rout.at[yp, s], rin.at[yp, s + 1], rsend.at[yp, s], rrecv.at[yp, s + 1], ctx=nxt)

    for yp in range(2):
        rout[yp, 1] = own_part(yp, (rank + 7) % NZ).astype(BF)
        chain(yp, 1).start()

    def hop(s, _):
        for yp in range(2):
            chain(yp, s - 1).wait_recv()
            rout[yp, s] = (own_part(yp, (rank - s + NZ) % NZ) + rin[yp, s].astype(F32)).astype(BF)
            chain(yp, s).start()
        return 0

    lax.fori_loop(2, NZ, hop, 0)
    for yp in range(2):
        chain(yp, NZ - 1).wait_recv()
    ys[...] = (own_part(1 - y, rank) + rin[1 - y, NZ].astype(F32)).astype(BF)
    y_copy = remote(ys, yr, ysem.at[0], ysem.at[1], ctx=ypart)
    y_copy.start()
    for step in range(1, TP):
        spread(step).wait_recv()

    acc = jnp.zeros((256, FEAT), F32)
    for step in range(1, TP):
        giver = (tp + TP - step) % TP
        got = gathered[giver]
        acc += dot(got[:, :128], wbuf[giver, 0], NT) + dot(got[:, 128:], wbuf[giver, 1], NT)
    dh_out[...] = (acc + total).astype(BF)

    y_copy.wait()
    final = own_part(y, rank) + rin[y, NZ].astype(F32) + yr[...].astype(F32)
    gk_out[...] = final[:, :128]
    gv_out[...] = final[:, 128:]
    for step in range(1, TP):
        spread(step).wait_send()

    def drain(s, _):
        for yp in range(2):
            chain(yp, s).wait_send()
        return 0

    lax.fori_loop(1, NZ, drain, 0)


def project(dk, dv, hid, wbuf, wko, wvo):
    vmem = pl.BlockSpec(memory_space=pltpu.VMEM)
    dma = pltpu.SemaphoreType.DMA
    sds = jax.ShapeDtypeStruct
    piece = (WROWS, 256)
    return pl.pallas_call(
        project_kernel,
        out_shape=[sds((WROWS, 128), F32), sds((WROWS, 128), F32), sds((256, FEAT), BF)],
        in_specs=[vmem] * 6,
        out_specs=[vmem] * 3,
        scratch_shapes=[
            pltpu.VMEM((256, 256), BF),
            pltpu.VMEM((TP, 256, 256), BF),
            pltpu.VMEM((5120, 256), F32),
            pltpu.VMEM((16,) + piece, BF),
            pltpu.VMEM((16,) + piece, BF),
            pltpu.VMEM((2, NZ + 1) + piece, BF),
            pltpu.VMEM((2, NZ) + piece, BF),
            pltpu.VMEM(piece, BF),
            pltpu.VMEM(piece, BF),
            dma((TP,)),
            dma((TP,)),
            dma((2,)),
            dma((2, NZ)),
            dma((2, NZ + 1)),
            dma((2,)),
        ],
        compiler_params=pltpu.CompilerParams(
            collective_id=1, has_side_effects=True, vmem_limit_bytes=48 * 2**20
        ),
        cost_estimate=pl.CostEstimate(flops=2 * 10**9, bytes_accessed=10**7, transcendentals=0),
    )(dk, dv, hid, wbuf, wko, wvo)


def shards(q, k, v, o, d, ln, order, hidden, wk, wv):
    i = lax.axis_index("ctx")
    swapped = jnp.full((8, 128), (order[2 * i] != i).astype(F32))
    dq, dk, dv, wbuf = attention(swapped, q, k, v, o, d, ln, wk, wv)
    tp = lax.axis_index("tp")
    wko = lax.dynamic_slice_in_dim(wk, tp * FEAT, FEAT, 0)
    wvo = lax.dynamic_slice_in_dim(wv, tp * FEAT, FEAT, 0)
    gk, gv, dh = project(dk, dv, hidden, wbuf, wko, wvo)
    return dq, dk, dv, gk, gv, dh


def solution(mesh):
    split = P("ctx", "tp")
    in_specs = (split,) * 5 + (P("tp", "ctx"), P(), P("ctx", None), P(None, "tp"), P(None, "tp"))
    return jax.shard_map(
        shards, mesh=mesh, in_specs=in_specs, out_specs=(split,) * 6, check_vma=False
    )
```

time: 753 us -> 126 us (0.17)
  waiting for transfers between devices: 307 us -> 0 us
  matrix products: 237 us -> 0 us
  Pallas kernels: 0 us -> 108 us
  local copies, waits for them, and re-layouts: 122 us -> 16.2 us
  loops' own time: 42.2 us -> 0 us
  between operations: 16.9 us -> 1.36 us
  starting transfers between devices: 14.5 us -> 0 us
    dot_general x163 -> x0, matrix products: 237 us -> none  [the longest x32 94.5 us: tile_grads(): jnp.einsum('hgqk,khd->qhgd', dscores_low, key_tile, preferred_element_typ...]
    unnamed x4 -> x0, waiting for transfers between devices: 188 us -> none
    ppermute x126 -> x0, waiting for transfers between devices: 119 us -> none  [shifted(): return lax.ppermute(value, axis, pairs)]
    pallas_call x0 -> x2, Pallas kernels: none -> 108 us  [the longest x1 67.3 us: attention(): pl.pallas_call(attention_kernel, out_shape=[sds((256, 1024), BF), sds((25...]
    while x187 -> x0, local copies, waits for them, and re-layouts: 72.4 us -> none
    another operation x1 -> x0, loops' own time: 42.2 us -> none  [shards(): lax.fori_loop(0, cycle_size - 1, cycle_step, (dq_start, key_act, value_ac...]
    slice x33 -> x0, local copies, waits for them, and re-layouts: 20.3 us -> none  [the longest x32 18.7 us: step_work(): source_spans[0] * span_len + offsets]
    ppermute x126 -> x0, starting transfers between devices: 14.4 us -> none  [shifted(): return lax.ppermute(value, axis, pairs)]
  transfers between devices with their start and end apart: 128 -> 0, of which waited for: 65 -> 0; matrix products, arithmetic and copies ran while one was open for 39% -> 0% of each run, Pallas kernels for 0% -> 0%
where the time goes in v1:
time: 126 us; the launch traced here: 125 us
  Pallas kernels  108 us (86%)
  local copies, waits for them, and re-layouts  16.2 us (13%)
  between operations  1.36 us (1%)
    pallas_call x1, Pallas kernels, attention(): pl.pallas_call(attention_kernel, out_shape=[sds((256, 1024), BF), sds((25...  67.3 us
    pallas_call x1, Pallas kernels, project(): pl.pallas_call(project_kernel, out_shape=[sds((WROWS, 128), F32), sds((WR...  40.3 us
    unnamed x26, local copies, waits for them, and re-layouts  13.9 us

profile of v1, /device:TPU:8, one launch (start us, length us, event | category | flops | bytes accessed | tf_op | source)
XLA Modules:
  0.0 125.2 jit_solution(3513387735351676130)
XLA Ops:
  0.6 1.2 dynamic_slice.9
  2.5 0.0 copy-start
  2.6 1.3 %copy-done = bf16[5120,128]{1,0:T(8,128)(2,1)S(1)} copy-done((bf16[5120,128]{1,0:T(8,128)(2,1)S(1)}, bf16[5120,128]{1,0:T(8,128)(2,1)}, u32[]{:S(2)}) %copy-start) | copy-done | bytes 1310744
  3.9 0.0 copy-start.1
  3.9 1.3 %copy-done.1 = bf16[5120,128]{1,0:T(8,128)(2,1)S(1)} copy-done((bf16[5120,128]{1,0:T(8,128)(2,1)S(1)}, bf16[5120,128]{1,0:T(8,128)(2,1)}, u32[]{:S(2)}) %copy-start.1) | copy-done | bytes 1310744
  5.2 0.0 copy-start.3
  5.2 1.0 copy-done.3
  6.2 0.0 copy-start.4
  6.2 1.0 copy-done.4
  7.3 0.0 copy-start.5
  7.3 1.0 copy-done.5
  8.3 0.0 copy-start.6
  8.3 0.8 copy-done.6
  9.1 0.0 copy-start.7
  9.1 0.8 copy-done.7
  10.0 0.0 copy-start.8
  10.0 0.7 copy-done.8
  10.7 0.0 copy-start.2
  10.7 67.3 %shard_map.145 = (bf16[256,1024]{1,0:T(8,128)(2,1)S(1)}, bf16[256,128]{1,0:T(8,128)(2,1)S(1)}, bf16[256,128]{1,0:T(8,128)(2,1)S(1)}, bf16[8,2,640,128]{3,2,1,0:T(8,128)(2,1)}) custom-call(f32[8,128]{1,0:T(8,128)S(1)} %broadcast_in_dim.3.swapped, bf16[256,1024]{1,0:T(8,128)(2,1)S(1)} %copy-done.3, bf16[256,128]{1,0:T(8,128)(2,1)S(1)} %copy-done.6, ...), custom_call_target="tpu_custom_call" | custom-call | flops 11000000512 | bytes 10000000 | tf_op jit(solution)/shard_map/pallas_call | solution.py:383
  78.0 1.0 constant_dynamic-slice_fusion
  79.1 0.0 copy-done.2
  79.1 0.0 copy-start.9
  79.1 1.7 %copy-done.9 = bf16[8,2,640,128]{3,2,1,0:T(8,128)(2,1)S(1)} copy-done((bf16[8,2,640,128]{3,2,1,0:T(8,128)(2,1)S(1)}, bf16[8,2,640,128]{3,2,1,0:T(8,128)(2,1)}, u32[]{:S(2)}) %copy-start.9) | copy-done | bytes 2621464
  80.8 40.3 %shard_map.146 = (f32[160,128]{1,0:T(8,128)S(1)}, f32[160,128]{1,0:T(8,128)S(1)}, bf16[256,640]{1,0:T(8,128)(2,1)S(1)}) custom-call(bf16[256,128]{1,0:T(8,128)(2,1)S(1)} %get-tuple-element.29.dk, bf16[256,128]{1,0:T(8,128)(2,1)S(1)} %get-tuple-element.30.dv, bf16[256,5120]{1,0:T(8,128)(2,1)S(1)} %copy-done.2, bf16[8,2,640,128]{3,2,1,0:T(8,128)(2,1)S(1)} %copy-done.9, ...), custom_call_target="tpu_custom_call" | custom-call | flops 2000000000 | bytes 10000000 | tf_op jit(solution)/shard_map/pallas_call | solution.py:540
  121.1 0.8 copy.22
  121.9 0.6 copy.23
  122.6 0.6 copy.24
  123.2 0.6 copy.25
  123.8 0.6 copy.26
  124.5 0.7 copy.27
  (1 shorter events, 0.0 us)
Async XLA Ops:
  2.5 1.3 %copy-start = (bf16[5120,128]{1,0:T(8,128)(2,1)S(1)}, bf16[5120,128]{1,0:T(8,128)(2,1)}, u32[]{:S(2)}) copy-start(bf16[5120,128]{1,0:T(8,128)(2,1)} %wk.1) | copy-start | bytes 3932164
  3.9 1.3 %copy-start.1 = (bf16[5120,128]{1,0:T(8,128)(2,1)S(1)}, bf16[5120,128]{1,0:T(8,128)(2,1)}, u32[]{:S(2)}) copy-start(bf16[5120,128]{1,0:T(8,128)(2,1)} %wv.1) | copy-start | bytes 3932164
  5.2 1.0 copy-start.3
  6.2 1.0 copy-start.4
  7.3 1.0 copy-start.5
  8.3 0.8 copy-start.6
  9.1 0.8 copy-start.7
  10.0 0.7 copy-start.8
  10.7 68.4 %copy-start.2 = (bf16[256,5120]{1,0:T(8,128)(2,1)S(1)}, bf16[256,5120]{1,0:T(8,128)(2,1)}, u32[]{:S(2)}) copy-start(bf16[256,5120]{1,0:T(8,128)(2,1)} %hid.1) | copy-start | bytes 7864324
  79.1 1.7 %copy-start.9 = (bf16[8,2,640,128]{3,2,1,0:T(8,128)(2,1)S(1)}, bf16[8,2,640,128]{3,2,1,0:T(8,128)(2,1)}, u32[]{:S(2)}) copy-start(bf16[8,2,640,128]{3,2,1,0:T(8,128)(2,1)} %get-tuple-element.16.wbuf) | copy-start | bytes 7864324

commit v2 on v1

v2 whole, which is shorter than its diff:
```python
import functools
import math

import jax
import jax.numpy as jnp
from jax import lax
from jax.experimental import pallas as pl
from jax.experimental.pallas import tpu as pltpu
from jax.sharding import PartitionSpec as P

BF = jnp.bfloat16
F32 = jnp.float32
MESH = pl.DeviceIdType.MESH
SCALE = 1.0 / math.sqrt(128)
LOG2E = math.log2(math.e)
NT = (((1,), (1,)), ((), ()))
TN = (((0,), (0,)), ((), ()))
SPAN = 128
TP = 8
NZ = 8
FEAT = 640
HALF_FEAT = 320
WROWS = 160

dot = functools.partial(lax.dot_general, preferred_element_type=F32)


def mm(a, b):
    return jnp.dot(a, b, preferred_element_type=F32)


def place():
    i = lax.axis_index("ctx")
    return i, i % 2, (i // 2) % NZ, i // 16


def ctx_of(y, z, core):
    return y * 16 + z * 2 + core


def remote(src, dst, send, recv, **where):
    return pltpu.make_async_remote_copy(
        src_ref=src, dst_ref=dst, send_sem=send, recv_sem=recv, device_id=where, device_id_type=MESH
    )


def kernel(
    swapped, q_hbm, k_hbm, v_hbm, o_hbm, d_hbm, ln_hbm, hid_hbm, wk, wv,
    dq_out, dk_out, dv_out, gk_out, gv_out, dh_out,
    q_in, k_in, v_in, o_in, d_in, ln_in, hid,
    qb, db, ob, lnc, lnb, deb, dqa, kv, acc, ysum_out, ysum_in, sum_out, sum_in, dqs, dqr,
    wbuf, dkv, gathered, part, cs, cr, gout, gin, fs, fr,
    lsem, xsend, xrecv, zsend, zrecv, ysend, yrecv, ysem_s, ysem_r, ssend, srecv,
    wsend, wrecv, fsend, frecv, dsem, tsend, trecv, csend, crecv, gsend, grecv,
):
    i, core, z, y = place()
    tp = lax.axis_index("tp")
    other = 1 - core
    chip = y * NZ + z
    odd = z % 2
    quad = z // 2
    ypart = ctx_of(1 - y, z, core)
    mate = ctx_of(y, z, other)

    def z_at(step):
        return (z + step + NZ) % NZ

    up_dev = ctx_of(y, z_at(1), core)
    down_dev = ctx_of(y, z_at(-1), core)
    reach = (3 + core, 4 - core)

    loads = [
        pltpu.make_async_copy(src, dst, lsem.at[n])
        for n, (src, dst) in enumerate(
            (
                (k_hbm, k_in), (v_hbm, v_in), (q_hbm, q_in), (d_hbm, d_in), (o_hbm, o_in),
                (ln_hbm, ln_in), (hid_hbm, hid),
                (wk.at[pl.ds(pl.multiple_of(tp * FEAT, FEAT), FEAT), :], wbuf.at[tp, 0]),
                (wv.at[pl.ds(pl.multiple_of(tp * FEAT, FEAT), FEAT), :], wbuf.at[tp, 1]),
            )
        )
    ]
    for load in loads:
        load.start()

    barrier = pltpu.get_barrier_semaphore()
    for dev in (ypart, mate):
        pl.semaphore_signal(barrier, inc=1, device_id={"ctx": dev}, device_id_type=MESH)
    for step in range(1, NZ):
        dev = ctx_of(y, z_at(step), core)
        pl.semaphore_signal(barrier, inc=1, device_id={"ctx": dev}, device_id_type=MESH)
        pl.semaphore_signal(
            barrier, inc=1, device_id={"tp": (tp + step) % TP}, device_id_type=MESH
        )

    flip_wide = jnp.concatenate([swapped[...]] * 16, axis=0)
    flip16 = flip_wide.astype(BF) > 0.5

    def canon(first, second, hl):
        return jnp.where(flip16, second, first) if hl == 0 else jnp.where(flip16, first, second)

    loads[0].wait()
    loads[1].wait()
    for hl in range(2):
        kv[y, z, 2 * hl] = canon(k_in[:SPAN, :], k_in[SPAN:, :], hl)
        kv[y, z, 2 * hl + 1] = canon(v_in[:SPAN, :], v_in[SPAN:, :], hl)
    pl.semaphore_wait(barrier, 2 * NZ)

    def hop(up, d):
        block = kv.at[y, z_at(-d if up else d)]
        return remote(
            block, block, zsend.at[up, d], zrecv.at[up, d + 1], ctx=up_dev if up else down_dev
        )

    def across(zz, act):
        @pl.when(y == 0)
        def _():
            block = kv.at[0, zz, 0:2]
            act(remote(block, block, ysend.at[zz], yrecv.at[zz], ctx=ypart))

        @pl.when(y == 1)
        def _():
            block = kv.at[1, zz]
            act(remote(block, block, ysend.at[zz], yrecv.at[zz], ctx=ypart))

    def across_wait(zz):
        @pl.when(y == 1)
        def _():
            block = kv.at[0, zz, 0:2]
            remote(block, block, ysend.at[zz], yrecv.at[zz], ctx=ypart).wait_recv()

        @pl.when(y == 0)
        def _():
            block = kv.at[1, zz]
            remote(block, block, ysend.at[zz], yrecv.at[zz], ctx=ypart).wait_recv()

    hop(1, 0).start()
    hop(0, 0).start()
    across(z, lambda copy: copy.start())

    for load in loads[2:6]:
        load.wait()
    for hl in range(2):
        for h in range(8):
            cols = slice(h * 128, (h + 1) * 128)
            for full, here in ((qb, q_in), (db, d_in), (ob, o_in)):
                full[core, hl, cols, :] = canon(here[:SPAN, cols], here[SPAN:, cols], hl)
    both = ln_in[...] * LOG2E
    flip8 = swapped[...] > 0.5
    lnc[core, 0] = jnp.where(flip8, both[:, SPAN:], both[:, :SPAN])
    lnc[core, 1] = jnp.where(flip8, both[:, :SPAN], both[:, SPAN:])
    swaps = [
        remote(ref.at[core], ref.at[core], xsend.at[n], xrecv.at[n], ctx=mate)
        for n, ref in enumerate((qb, db, ob, lnc))
    ]
    for swap in swaps:
        swap.start()

    def zero(n, _):
        for at in range(4):
            acc[n // NZ, n % NZ, at] = jnp.zeros((128, 128), F32)
        return 0

    lax.fori_loop(0, 2 * NZ, zero, 0)
    dqa[...] = jnp.zeros_like(dqa)

    ones = jnp.ones((128, 128), BF)
    head_of = lax.broadcasted_iota(jnp.int32, (32, 1024), 1) // 128
    pick = (lax.broadcasted_iota(jnp.int32, (32, 1024), 0) % 8 == head_of).astype(F32).astype(BF)

    def row_terms(slot):
        for hl in range(2):
            prod = db[slot, hl].astype(F32) * ob[slot, hl].astype(F32)
            high = prod.astype(BF)
            low = (prod - high.astype(F32)).astype(BF)
            deb[slot, hl] = mm(high, ones) + mm(low, ones)
            norm = lnc[slot, hl]
            p1 = norm.astype(BF)
            rest = norm - p1.astype(F32)
            p2 = rest.astype(BF)
            rest = rest - p2.astype(F32)
            p3 = rest.astype(BF)
            parts = jnp.concatenate(
                [p1.astype(F32), p2.astype(F32), p3.astype(F32), jnp.zeros((8, 128), F32)], axis=0
            ).astype(BF)
            wide = dot(parts, pick, TN)
            for h in range(8):
                lnb[slot, hl, h * 128 : (h + 1) * 128, :] = wide[:, h * 128 : (h + 1) * 128]

    row_terms(core)

    def pump(d):
        for up in (1, 0):

            @pl.when(d <= reach[up])
            def _():
                hop(up, d - 1).wait_recv()

                @pl.when(d < reach[up])
                def _():
                    hop(up, d).start()

                across(z_at(-d if up else d), lambda copy: copy.start())

    for swap in swaps:
        swap.wait()
    row_terms(other)
    pump(1)

    def unit(yp, w, hk, hq, masked):
        ra = 2 * w
        rb = 2 * w + 1
        k = jnp.concatenate([kv[yp, ra, 2 * hk], kv[yp, rb, 2 * hk]], axis=0)
        v = jnp.concatenate([kv[yp, ra, 2 * hk + 1], kv[yp, rb, 2 * hk + 1]], axis=0)
        gk = None
        gv = None
        for slot in range(2):
            q = qb[slot, hq]
            d = db[slot, hq]
            ln = lnb[slot, hq]
            de = deb[slot, hq]
            scores = dot(q, k, NT)
            dp = dot(d, v, NT)
            prob = jnp.exp2(scores * (SCALE * LOG2E) - jnp.concatenate([ln, ln], axis=1))
            if masked:
                qi = 2 * chip + slot
                qspan = jnp.where(hq == 0, qi, 63 - qi)
                shape = (1024, 128)
                gap = (
                    lax.broadcasted_iota(jnp.int32, shape, 0) % SPAN
                    - lax.broadcasted_iota(jnp.int32, shape, 1)
                )
                seen = []
                for rk in (ra, rb):
                    ki = 2 * (yp * NZ + rk) + core
                    kspan = jnp.where(hk == 0, ki, 63 - ki)
                    seen.append(gap >= (kspan - qspan) * SPAN)
                prob = jnp.concatenate(
                    [
                        jnp.where(seen[0], prob[:, :128], 0.0),
                        jnp.where(seen[1], prob[:, 128:], 0.0),
                    ],
                    axis=1,
                )
            ds = (prob * (dp - jnp.concatenate([de, de], axis=1))).astype(BF)
            pr = prob.astype(BF)
            dqa[slot, hq] += mm(ds, k)
            gk = dot(q, ds, TN) if gk is None else gk + dot(q, ds, TN)
            gv = dot(d, pr, TN) if gv is None else gv + dot(d, pr, TN)
        acc[yp, ra, 2 * hk] += gk[:, :128]
        acc[yp, rb, 2 * hk] += gk[:, 128:]
        acc[yp, ra, 2 * hk + 1] += gv[:, :128]
        acc[yp, rb, 2 * hk + 1] += gv[:, 128:]

    def pair_at(n):
        near = jnp.where(n == 1, 2 * odd - 1, 1 - 2 * odd)
        return (quad + jnp.where(n == 0, 0, jnp.where(n == 3, 2, near)) + 4) % 4

    def sum_across(zz, act):
        @pl.when(y == 0)
        def _():
            act(remote(ysum_out.at[zz], ysum_in.at[zz], ysem_s.at[zz], ysem_r.at[zz], ctx=ypart))

        @pl.when(y == 1)
        def _():
            src, dst = ysum_out.at[zz, 0:2], ysum_in.at[zz, 0:2]
            act(remote(src, dst, ysem_s.at[zz], ysem_r.at[zz], ctx=ypart))

    def sum_across_wait(zz):
        @pl.when(y == 1)
        def _():
            remote(
                ysum_out.at[zz], ysum_in.at[zz], ysem_s.at[zz], ysem_r.at[zz], ctx=ypart
            ).wait_recv()

        @pl.when(y == 0)
        def _():
            src, dst = ysum_out.at[zz, 0:2], ysum_in.at[zz, 0:2]
            remote(src, dst, ysem_s.at[zz], ysem_r.at[zz], ctx=ypart).wait_recv()

    def sum_home(zz):
        return remote(
            sum_out.at[zz], sum_in.at[z], ssend.at[zz], srecv.at[z], ctx=ctx_of(y, zz, core)
        )

    def send_across(n):
        w = pair_at(n)
        for zz in (2 * w, 2 * w + 1):
            ysum_out[zz] = acc[1 - y, zz].astype(BF)
            sum_across(zz, lambda copy: copy.start())

    def add_across(zz):
        sum_across_wait(zz)
        acc[y, zz, 0:2] += ysum_in[zz, 0:2].astype(F32)

        @pl.when(y == 1)
        def _():
            acc[y, zz, 2:4] += ysum_in[zz, 2:4].astype(F32)

    def send_home(n):
        w = pair_at(n)
        for zz in (2 * w, 2 * w + 1):
            add_across(zz)

            @pl.when(zz != z)
            def _():
                sum_out[zz] = acc[y, zz].astype(BF)
                sum_home(zz).start()

    def weight_copies(step):
        peer = (tp + step) % TP
        out = []
        for n, ref in enumerate((wk, wv)):
            rows = pl.ds(pl.multiple_of(peer * FEAT + core * HALF_FEAT, 64), HALF_FEAT)
            mine = pl.ds(pl.multiple_of(core * HALF_FEAT, 64), HALF_FEAT)
            out.append(
                remote(
                    ref.at[rows, :], wbuf.at[tp, n, mine, :],
                    wsend.at[step, n], wrecv.at[step, n], tp=peer,
                )
            )
        return out

    def weight_forwards(step):
        giver = (tp + TP - step) % TP
        out = []
        for n in range(2):
            mine = pl.ds(pl.multiple_of(core * HALF_FEAT, 64), HALF_FEAT)
            block = wbuf.at[giver, n, mine, :]
            out.append(remote(block, block, fsend.at[step, n], frecv.at[step, n], ctx=mate))
        return out

    def half_step(x, _):
        n = x // 2
        w = pair_at(n)
        far = jnp.where(x >= 6, 1 - x % 2, x % 2)
        yp = (y + far) % 2

        @pl.when(far == 1)
        def _():
            across_wait(2 * w)
            across_wait(2 * w + 1)

        @pl.when(x > 0)
        def _():
            for copy in weight_copies(x):
                copy.start()

        unit(yp, w, 0, 1, False)
        own = jnp.logical_and(far == 0, n == 0)

        @pl.when(own)
        def _():
            def masked_unit(hl, _):
                unit(yp, w, hl, hl, True)
                return 0

            lax.fori_loop(0, 2, masked_unit, 0)

        @pl.when(jnp.logical_not(own))
        def _():
            hl = jnp.where(yp * NZ + 2 * w < chip, 0, 1)
            unit(yp, w, hl, hl, False)

        @pl.when(far == 1)
        def _():
            send_across(n)

        for at, d in ((0, 2), (2, 3), (4, 4)):

            @pl.when(x == at)
            def _():
                pump(d)

        for at, done in ((3, 0), (5, 1), (6, 2), (7, 3)):

            @pl.when(x == at)
            def _():
                send_home(done)

        @pl.when(x > 1)
        def _():
            for copy in weight_copies(x - 1):
                copy.wait_recv()
            for copy in weight_forwards(x - 1):
                copy.start()

        return 0

    lax.fori_loop(0, 8, half_step, 0)

    dqs[...] = (dqa[other] * SCALE).astype(BF)
    dq_copy = remote(dqs, dqr, dsem.at[0], dsem.at[1], ctx=mate)
    dq_copy.start()
    for copy in weight_copies(TP - 1):
        copy.wait_recv()
    for copy in weight_forwards(TP - 1):
        copy.start()
    dq_copy.wait()
    for h in range(8):
        cols = slice(h * 128, (h + 1) * 128)
        low = (dqa[core, 0, cols, :] * SCALE + dqr[0, cols, :].astype(F32)).astype(BF)
        high = (dqa[core, 1, cols, :] * SCALE + dqr[1, cols, :].astype(F32)).astype(BF)
        dq_out[0:SPAN, cols] = jnp.where(flip16, high, low)
        dq_out[SPAN:, cols] = jnp.where(flip16, low, high)

    def collect(step, _):
        zz = z_at(step)
        remote(sum_out.at[zz], sum_in.at[zz], ssend.at[zz], srecv.at[zz], ctx=mate).wait_recv()
        for at in range(4):
            acc[y, z, at] += sum_in[zz, at].astype(F32)
        return 0

    lax.fori_loop(1, NZ, collect, 0)
    for out, at, factor in ((dk_out, 0, SCALE), (dv_out, 1, 1.0)):
        low = (acc[y, z, at] * factor).T.astype(BF)
        high = (acc[y, z, at + 2] * factor).T.astype(BF)
        cols = slice(at * 128, (at + 1) * 128)
        for rows, value in (
            (slice(0, SPAN), jnp.where(flip16, high, low)),
            (slice(SPAN, 2 * SPAN), jnp.where(flip16, low, high)),
        ):
            out[rows, :] = value
            dkv[rows, cols] = value

    def spread(step):
        return remote(dkv, gathered.at[tp], tsend.at[step], trecv.at[step], tp=(tp + step) % TP)

    for step in range(1, TP):
        spread(step).start()

    mine = dkv[...]
    loads[6].wait()

    def rows_of(yp, zz, k):
        return pl.ds(pl.multiple_of(((yp * NZ + zz) * 2 + k) * WROWS, 32), WROWS)

    def swap_part(yp):
        return remote(cs.at[yp], cr.at[yp], csend.at[yp], crecv.at[yp], ctx=mate)

    for yp in range(2):
        for n in range(5):
            at = yp * 2560 + n * 512
            part[at : at + 512, :] = dot(hid[:, at : at + 512], mine, TN)

        def fill(zz, _):
            cs[yp, zz] = part[rows_of(yp, zz, other), :].astype(BF)
            return 0

        lax.fori_loop(0, NZ, fill, 0)
        swap_part(yp).start()
    for yp in range(2):
        swap_part(yp).wait()

    def own_part(yp, zz):
        return part[rows_of(yp, zz, core), :] + cr[yp, zz].astype(F32)

    def arm(up, a, yp):
        return remote(
            gout.at[up, a, yp], gin.at[up, a - 1, yp],
            gsend.at[up, a, yp], grecv.at[up, a - 1, yp],
            ctx=up_dev if up else down_dev,
        )

    def arms(k, _):
        a = 4 - k
        for turn in range(2):
            yp = (1 - y) if turn == 0 else y
            for up in (1, 0):
                zz = (z + a) % NZ if up else (z - a + NZ) % NZ

                @pl.when(a == reach[up])
                def _():
                    gout[up, a, yp] = own_part(yp, zz).astype(BF)

                @pl.when(a < reach[up])
                def _():
                    arm(up, a + 1, yp).wait_recv()
                    gout[up, a, yp] = (own_part(yp, zz) + gin[up, a, yp].astype(F32)).astype(BF)

                @pl.when(a <= reach[up])
                def _():
                    arm(up, a, yp).start()

        return 0

    lax.fori_loop(0, 4, arms, 0)

    def plane_sum(yp):
        arm(1, 1, yp).wait_recv()
        arm(0, 1, yp).wait_recv()
        return own_part(yp, z) + gin[1, 0, yp].astype(F32) + gin[0, 0, yp].astype(F32)

    fs[...] = plane_sum(1 - y).astype(BF)
    f_copy = remote(fs, fr, dsem.at[2], dsem.at[3], ctx=ypart)
    f_copy.start()
    final = plane_sum(y)

    gathered[tp] = mine
    loads[7].wait()
    loads[8].wait()
    for step in range(1, TP):
        for copy in weight_forwards(step):
            copy.wait()
        spread(step).wait_recv()
    total = None
    for giver in range(TP):
        got = gathered[giver]
        term = dot(got[:, :128], wbuf[giver, 0], NT) + dot(got[:, 128:], wbuf[giver, 1], NT)
        total = term if total is None else total + term
    dh_out[...] = total.astype(BF)

    f_copy.wait()
    final = final + fr[...].astype(F32)
    gk_out[...] = final[:, :128]
    gv_out[...] = final[:, 128:]

    def drain(s, _):
        across(s, lambda copy: copy.wait_send())
        sum_across(s, lambda copy: copy.wait_send())

        @pl.when(s > 0)
        def _():
            for copy in weight_copies(s):
                copy.wait_send()
            sum_home(z_at(s)).wait_send()
            spread(s).wait_send()

        for up in (0, 1):

            @pl.when(s < reach[up])
            def _():
                hop(up, s).wait_send()
                for yp in range(2):
                    arm(up, s + 1, yp).wait_send()

        return 0

    lax.fori_loop(0, NZ, drain, 0)


def backward(*args):
    vmem = pl.BlockSpec(memory_space=pltpu.VMEM)
    hbm = pl.BlockSpec(memory_space=pl.ANY)
    dma = pltpu.SemaphoreType.DMA
    sds = jax.ShapeDtypeStruct
    rows = (2, 2, 1024, 128)
    block = (4, 128, 128)
    piece = (WROWS, 256)
    return pl.pallas_call(
        kernel,
        out_shape=[
            sds((256, 1024), BF),
            sds((256, 128), BF),
            sds((256, 128), BF),
            sds((WROWS, 128), F32),
            sds((WROWS, 128), F32),
            sds((256, FEAT), BF),
        ],
        in_specs=[vmem] + [hbm] * 9,
        out_specs=[vmem] * 6,
        scratch_shapes=[
            pltpu.VMEM((256, 1024), BF),
            pltpu.VMEM((256, 128), BF),
            pltpu.VMEM((256, 128), BF),
            pltpu.VMEM((256, 1024), BF),
            pltpu.VMEM((256, 1024), BF),
            pltpu.VMEM((8, 256), F32),
            pltpu.VMEM((256, 5120), BF),
            pltpu.VMEM(rows, BF),
            pltpu.VMEM(rows, BF),
            pltpu.VMEM(rows, BF),
            pltpu.VMEM((2, 2, 8, 128), F32),
            pltpu.VMEM(rows, F32),
            pltpu.VMEM(rows, F32),
            pltpu.VMEM(rows, F32),
            pltpu.VMEM((2, NZ) + block, BF),
            pltpu.VMEM((2, NZ) + block, F32),
            pltpu.VMEM((NZ,) + block, BF),
            pltpu.VMEM((NZ,) + block, BF),
            pltpu.VMEM((NZ,) + block, BF),
            pltpu.VMEM((NZ,) + block, BF),
            pltpu.VMEM((2, 1024, 128), BF),
            pltpu.VMEM((2, 1024, 128), BF),
            pltpu.VMEM((TP, 2, FEAT, 128), BF),
            pltpu.VMEM((256, 256), BF),
            pltpu.VMEM((TP, 256, 256), BF),
            pltpu.VMEM((5120, 256), F32),
            pltpu.VMEM((2, NZ) + piece, BF),
            pltpu.VMEM((2, NZ) + piece, BF),
            pltpu.VMEM((2, 5, 2) + piece, BF),
            pltpu.VMEM((2, 4, 2) + piece, BF),
            pltpu.VMEM(piece, BF),
            pltpu.VMEM(piece, BF),
            dma((9,)),
            dma((4,)),
            dma((4,)),
            dma((2, 5)),
            dma((2, 5)),
            dma((NZ,)),
            dma((NZ,)),
            dma((NZ,)),
            dma((NZ,)),
            dma((NZ,)),
            dma((NZ,)),
            dma((TP, 2)),
            dma((TP, 2)),
            dma((TP, 2)),
            dma((TP, 2)),
            dma((4,)),
            dma((TP,)),
            dma((TP,)),
            dma((2,)),
            dma((2,)),
            dma((2, 5, 2)),
            dma((2, 5, 2)),
        ],
        compiler_params=pltpu.CompilerParams(
            collective_id=0, has_side_effects=True, vmem_limit_bytes=58 * 2**20
        ),
        cost_estimate=pl.CostEstimate(
            flops=12 * 10**9, bytes_accessed=10**7, transcendentals=9 * 10**6
        ),
    )(*args)


def shards(q, k, v, o, d, ln, order, hidden, wk, wv):
    i = lax.axis_index("ctx")
    swapped = jnp.full((8, 128), (order[2 * i] != i).astype(F32))
    return tuple(backward(swapped, q, k, v, o, d, ln, hidden, wk, wv))


def solution(mesh):
    split = P("ctx", "tp")
    in_specs = (split,) * 5 + (P("tp", "ctx"), P(), P("ctx", None), P(None, "tp"), P(None, "tp"))
    return jax.shard_map(
        shards, mesh=mesh, in_specs=in_specs, out_specs=(split,) * 6, check_vma=False
    )
```

time: 126 us -> 116 us (0.921)
  local copies, waits for them, and re-layouts: 16.2 us -> 8.71 us
  Pallas kernels: 108 us -> 104 us
    unnamed x26 -> x12, local copies, waits for them, and re-layouts: 13.9 us -> 6.87 us
    pallas_call x2 -> x1, Pallas kernels: 108 us -> 104 us  [backward(): pl.pallas_call(kernel, out_shape=[sds((256, 1024), BF), sds((256, 128), B...]
where the time goes in v2:
time: 116 us; the launch traced here: 114 us
  Pallas kernels  104 us (90%)
  local copies, waits for them, and re-layouts  8.71 us (8%)
  between operations  1.33 us (1%)
    pallas_call x1, Pallas kernels, backward(): pl.pallas_call(kernel, out_shape=[sds((256, 1024), BF), sds((256, 128), B...  104 us
    unnamed x12, local copies, waits for them, and re-layouts  6.87 us

profile of v2, /device:TPU:8, one launch (start us, length us, event | category | flops | bytes accessed | tf_op | source)
XLA Modules:
  0.0 114.5 jit_solution(10830116468996227888)
XLA Ops:
  0.6 1.2 %dynamic_slice.3 = s32[1]{0:T(128)} dynamic-slice(s32[64]{0:T(128)} %param.16, s32[]{:T(128)S(6)} %select_n.3), dynamic_slice_sizes={1} | dynamic-slice | bytes 12 | tf_op jit(solution)/shard_map/dynamic_slice | solution.py:629
  2.5 0.6 broadcast_in_dim.3.swapped
  3.1 104.5 %shard_map.145 = (bf16[256,1024]{1,0:T(8,128)(2,1)}, bf16[256,128]{1,0:T(8,128)(2,1)}, bf16[256,128]{1,0:T(8,128)(2,1)}, f32[160,128]{1,0:T(8,128)}, f32[160,128]{1,0:T(8,128)}, /*index=5*/bf16[256,640]{1,0:T(8,128)(2,1)}) custom-call(f32[8,128]{1,0:T(8,128)} %broadcast_in_dim.3.swapped, bf16[256,1024]{1,0:T(8,128)(2,1)} %q_hbm.1, bf16[256,128]{1,0:T(8,128)(2,1)} %k_hbm.1, ...), custom_call_target="tpu_custom_call" | custom-call | flops 12000000000 | bytes 10000000 | tf_op jit(solution)/shard_map/pallas_call | solution.py:550
  107.6 0.0 copy-start.2
  107.6 0.0 copy-start.1
  107.6 0.0 copy-start
  107.6 1.9 %copy.22 = bf16[256,1024]{1,0:T(8,128)(2,1)} copy(bf16[256,1024]{1,0:T(8,128)(2,1)} %get-tuple-element.12) | data formatting | bytes 1048576
  109.5 1.5 %copy.23 = bf16[256,128]{1,0:T(8,128)(2,1)} copy(bf16[256,128]{1,0:T(8,128)(2,1)} %get-tuple-element.13) | data formatting | bytes 131072
  111.0 1.5 %copy.24 = bf16[256,128]{1,0:T(8,128)(2,1)} copy(bf16[256,128]{1,0:T(8,128)(2,1)} %get-tuple-element.14) | data formatting | bytes 131072
  112.5 0.0 copy-done.2
  112.5 0.6 copy.25
  113.1 0.0 copy-done.1
  113.1 0.6 copy.26
  113.8 0.0 copy-done
  113.8 0.7 copy.27
Async XLA Ops:
  107.6 4.9 %copy-start.2 = (f32[160,128]{1,0:T(8,128)S(1)}, f32[160,128]{1,0:T(8,128)}, u32[]{:S(2)}) copy-start(f32[160,128]{1,0:T(8,128)} %get-tuple-element.15) | copy-start | bytes 245764
  107.6 5.5 %copy-start.1 = (f32[160,128]{1,0:T(8,128)S(1)}, f32[160,128]{1,0:T(8,128)}, u32[]{:S(2)}) copy-start(f32[160,128]{1,0:T(8,128)} %get-tuple-element.16) | copy-start | bytes 245764
  107.6 6.2 %copy-start = (bf16[256,640]{1,0:T(8,128)(2,1)S(1)}, bf16[256,640]{1,0:T(8,128)(2,1)}, u32[]{:S(2)}) copy-start(bf16[256,640]{1,0:T(8,128)(2,1)} %get-tuple-element.17) | copy-start | bytes 983044

commit v3 on v2

--- a/solution.py
+++ b/solution.py
@@ -45,7 +45,7 @@
 
 
 def kernel(
-    swapped, q_hbm, k_hbm, v_hbm, o_hbm, d_hbm, ln_hbm, hid_hbm, wk, wv,
+    order, q_hbm, k_hbm, v_hbm, o_hbm, d_hbm, ln_hbm, hid_hbm, wk, wv,
     dq_out, dk_out, dv_out, gk_out, gv_out, dh_out,
     q_in, k_in, v_in, o_in, d_in, ln_in, hid,
     qb, db, ob, lnc, lnb, deb, dqa, kv, acc, ysum_out, ysum_in, sum_out, sum_in, dqs, dqr,
@@ -89,11 +89,15 @@
     for step in range(1, NZ):
         dev = ctx_of(y, z_at(step), core)
         pl.semaphore_signal(barrier, inc=1, device_id={"ctx": dev}, device_id_type=MESH)
-        pl.semaphore_signal(
-            barrier, inc=1, device_id={"tp": (tp + step) % TP}, device_id_type=MESH
-        )
-
-    flip_wide = jnp.concatenate([swapped[...]] * 16, axis=0)
+        peer = (tp + step) % TP
+        pl.semaphore_signal(barrier, inc=1, device_id={"tp": peer}, device_id_type=MESH)
+        if step % 2:
+            pl.semaphore_signal(
+                barrier, inc=1, device_id={"ctx": ypart, "tp": peer}, device_id_type=MESH
+            )
+
+    flip8 = jnp.full((8, 128), order[2 * i], jnp.int32) != jnp.full((8, 128), i, jnp.int32)
+    flip_wide = jnp.concatenate([jnp.where(flip8, 1.0, 0.0)] * 16, axis=0)
     flip16 = flip_wide.astype(BF) > 0.5
 
     def canon(first, second, hl):
@@ -104,7 +108,7 @@
     for hl in range(2):
         kv[y, z, 2 * hl] = canon(k_in[:SPAN, :], k_in[SPAN:, :], hl)
         kv[y, z, 2 * hl + 1] = canon(v_in[:SPAN, :], v_in[SPAN:, :], hl)
-    pl.semaphore_wait(barrier, 2 * NZ)
+    pl.semaphore_wait(barrier, 2 * NZ + TP // 2)
 
     def hop(up, d):
         block = kv.at[y, z_at(-d if up else d)]
@@ -146,7 +150,6 @@
             for full, here in ((qb, q_in), (db, d_in), (ob, o_in)):
                 full[core, hl, cols, :] = canon(here[:SPAN, cols], here[SPAN:, cols], hl)
     both = ln_in[...] * LOG2E
-    flip8 = swapped[...] > 0.5
     lnc[core, 0] = jnp.where(flip8, both[:, SPAN:], both[:, :SPAN])
     lnc[core, 1] = jnp.where(flip8, both[:, :SPAN], both[:, SPAN:])
     swaps = [
@@ -202,10 +205,11 @@
 
                 across(z_at(-d if up else d), lambda copy: copy.start())
 
+    pump(1)
     for swap in swaps:
         swap.wait()
     row_terms(other)
-    pump(1)
+    pump(2)
 
     def unit(yp, w, hk, hq, masked):
         ra = 2 * w
@@ -253,8 +257,8 @@
         acc[yp, rb, 2 * hk + 1] += gv[:, 128:]
 
     def pair_at(n):
-        near = jnp.where(n == 1, 2 * odd - 1, 1 - 2 * odd)
-        return (quad + jnp.where(n == 0, 0, jnp.where(n == 3, 2, near)) + 4) % 4
+        near = jnp.where(n == 2, 1 - 2 * odd, 2 * odd - 1)
+        return (quad + jnp.where(n == 0, 0, jnp.where(n == 1, 2, near)) + 4) % 4
 
     def sum_across(zz, act):
         @pl.when(y == 0)
@@ -316,7 +320,7 @@
             out.append(
                 remote(
                     ref.at[rows, :], wbuf.at[tp, n, mine, :],
-                    wsend.at[step, n], wrecv.at[step, n], tp=peer,
+                    wsend.at[step, n], wrecv.at[step, n], tp=peer, ctx=jnp.where(step % 2 == 1, ypart, i),
                 )
             )
         return out
@@ -331,9 +335,9 @@
         return out
 
     def half_step(x, _):
-        n = x // 2
+        n = jnp.where(x < 4, x // 2, 2 + x % 2)
         w = pair_at(n)
-        far = jnp.where(x >= 6, 1 - x % 2, x % 2)
+        far = jnp.where(x < 4, x % 2, jnp.where(x < 6, 1, 0))
         yp = (y + far) % 2
 
         @pl.when(far == 1)
@@ -341,9 +345,9 @@
             across_wait(2 * w)
             across_wait(2 * w + 1)
 
-        @pl.when(x > 0)
-        def _():
-            for copy in weight_copies(x):
+        @pl.when(x < 7)
+        def _():
+            for copy in weight_copies(x + 1):
                 copy.start()
 
         unit(yp, w, 0, 1, False)
@@ -366,7 +370,7 @@
         def _():
             send_across(n)
 
-        for at, d in ((0, 2), (2, 3), (4, 4)):
+        for at, d in ((0, 3), (1, 4)):
 
             @pl.when(x == at)
             def _():
@@ -438,10 +442,11 @@
     def swap_part(yp):
         return remote(cs.at[yp], cr.at[yp], csend.at[yp], crecv.at[yp], ctx=mate)
 
-    for yp in range(2):
+    for turn in range(2):
+        yp = (1 - y) if turn == 0 else y
         for n in range(5):
-            at = yp * 2560 + n * 512
-            part[at : at + 512, :] = dot(hid[:, at : at + 512], mine, TN)
+            at = pl.ds(pl.multiple_of(yp * 2560 + n * 512, 512), 512)
+            part[at, :] = dot(hid[:, at], mine, TN)
 
         def fill(zz, _):
             cs[yp, zz] = part[rows_of(yp, zz, other), :].astype(BF)
@@ -449,9 +454,6 @@
 
         lax.fori_loop(0, NZ, fill, 0)
         swap_part(yp).start()
-    for yp in range(2):
-        swap_part(yp).wait()
-
     def own_part(yp, zz):
         return part[rows_of(yp, zz, core), :] + cr[yp, zz].astype(F32)
 
@@ -466,6 +468,11 @@
         a = 4 - k
         for turn in range(2):
             yp = (1 - y) if turn == 0 else y
+
+            @pl.when(k == 0)
+            def _():
+                swap_part(yp).wait()
+
             for up in (1, 0):
                 zz = (z + a) % NZ if up else (z - a + NZ) % NZ
 
@@ -557,7 +564,7 @@
             sds((WROWS, 128), F32),
             sds((256, FEAT), BF),
         ],
-        in_specs=[vmem] + [hbm] * 9,
+        in_specs=[pl.BlockSpec(memory_space=pltpu.SMEM)] + [hbm] * 9,
         out_specs=[vmem] * 6,
         scratch_shapes=[
             pltpu.VMEM((256, 1024), BF),
@@ -624,10 +631,34 @@
     )(*args)
 
 
+def copy_kernel(*refs):
+    sems = refs[18]
+    inward = [pltpu.make_async_copy(refs[n], refs[12 + n], sems.at[0, n]) for n in range(6)]
+    outward = [pltpu.make_async_copy(refs[12 + n], refs[6 + n], sems.at[1, n]) for n in range(6)]
+    for copy in inward:
+        copy.start()
+    for n in range(6):
+        inward[n].wait()
+        outward[n].start()
+    for copy in outward:
+        copy.wait()
+
+
+def place_outputs(*outs):
+    hbm = pl.BlockSpec(memory_space=pl.ANY)
+    return pl.pallas_call(
+        copy_kernel,
+        out_shape=[jax.ShapeDtypeStruct(a.shape, a.dtype) for a in outs],
+        in_specs=[hbm] * 6,
+        out_specs=[hbm] * 6,
+        scratch_shapes=[pltpu.VMEM(a.shape, a.dtype) for a in outs]
+        + [pltpu.SemaphoreType.DMA((2, 6))],
+        compiler_params=pltpu.CompilerParams(vmem_limit_bytes=60 * 2**20),
+    )(*outs)
+
+
 def shards(q, k, v, o, d, ln, order, hidden, wk, wv):
-    i = lax.axis_index("ctx")
-    swapped = jnp.full((8, 128), (order[2 * i] != i).astype(F32))
-    return tuple(backward(swapped, q, k, v, o, d, ln, hidden, wk, wv))
+    return tuple(place_outputs(*backward(order, q, k, v, o, d, ln, hidden, wk, wv)))
 
 
 def solution(mesh):

time: 116 us -> 98.2 us (0.85)
  local copies, waits for them, and re-layouts: 8.71 us -> 0 us
  Pallas kernels: 104 us -> 96.4 us
    pallas_call x1, Pallas kernels: 104 us -> 94.3 us  [backward(): pl.pallas_call(kernel, out_shape=[sds((256, 1024), BF), sds((256, 128), B...]
    unnamed x12 -> x0, local copies, waits for them, and re-layouts: 6.87 us -> none
    pallas_call x0 -> x1, Pallas kernels: none -> 2.14 us  [place_outputs(): pl.pallas_call(copy_kernel, out_shape=[jax.ShapeDtypeStruct(a.shape, a.dt...]
    dynamic_slice x1 -> x0, local copies, waits for them, and re-layouts: 1.24 us -> none  [shards(): swapped = jnp.full((8, 128), (order[2 * i] != i).astype(F32))]
where the time goes in v3:
time: 98.2 us; the launch traced here: 97.1 us
  Pallas kernels  96.4 us (98%)
    pallas_call x1, Pallas kernels, backward(): pl.pallas_call(kernel, out_shape=[sds((256, 1024), BF), sds((256, 128), B...  94.3 us
    pallas_call x1, Pallas kernels, place_outputs(): pl.pallas_call(copy_kernel, out_shape=[jax.ShapeDtypeStruct(a.shape, a.dt...  2.14 us

profile of v3, /device:TPU:8, one launch (start us, length us, event | category | flops | bytes accessed | tf_op | source)
XLA Modules:
  0.0 97.1 jit_solution(11308212356732965536)
XLA Ops:
  0.6 94.3 %shard_map.145 = (bf16[256,1024]{1,0:T(8,128)(2,1)}, bf16[256,128]{1,0:T(8,128)(2,1)}, bf16[256,128]{1,0:T(8,128)(2,1)}, f32[160,128]{1,0:T(8,128)}, f32[160,128]{1,0:T(8,128)}, /*index=5*/bf16[256,640]{1,0:T(8,128)(2,1)}) custom-call(s32[64]{0:T(128)} %order.1, bf16[256,1024]{1,0:T(8,128)(2,1)} %q_hbm.1, bf16[256,128]{1,0:T(8,128)(2,1)} %k_hbm.1, ...), custom_call_target="tpu_custom_call" | custom-call | flops 12000000000 | bytes 10000000 | tf_op jit(solution)/shard_map/pallas_call | solution.py:557
  94.9 2.1 %shard_map.146 = (bf16[256,1024]{1,0:T(8,128)(2,1)}, bf16[256,128]{1,0:T(8,128)(2,1)}, bf16[256,128]{1,0:T(8,128)(2,1)}, f32[160,128]{1,0:T(8,128)}, f32[160,128]{1,0:T(8,128)}, /*index=5*/bf16[256,640]{1,0:T(8,128)(2,1)}) custom-call(bf16[256,1024]{1,0:T(8,128)(2,1)} %get-tuple-element.12.refs_0_, bf16[256,128]{1,0:T(8,128)(2,1)} %get-tuple-element.13.refs_1_, ...), custom_call_target="tpu_custom_call" | custom-call | tf_op jit(solution)/shard_map/pallas_call | solution.py:649

commit v4 on v3

--- a/solution.py
+++ b/solution.py
@@ -48,9 +48,9 @@
     order, q_hbm, k_hbm, v_hbm, o_hbm, d_hbm, ln_hbm, hid_hbm, wk, wv,
     dq_out, dk_out, dv_out, gk_out, gv_out, dh_out,
     q_in, k_in, v_in, o_in, d_in, ln_in, hid,
-    qb, db, ob, lnc, lnb, deb, dqa, kv, acc, ysum_out, ysum_in, sum_out, sum_in, dqs, dqr,
+    qb, db, ob, lnc, lnb, deb, dqa, kv, acc, ysum_out, ysum_in, sum_out, sum_in, home_in, dqs, dqr,
     wbuf, dkv, gathered, part, cs, cr, gout, gin, fs, fr,
-    lsem, xsend, xrecv, zsend, zrecv, ysend, yrecv, ysem_s, ysem_r, ssend, srecv,
+    lsem, xsend, xrecv, zsend, zrecv, ysend, yrecv, ysem_s, ysem_r, ssend, srecv, homer,
     wsend, wrecv, fsend, frecv, dsem, tsend, trecv, csend, crecv, gsend, grecv,
 ):
     i, core, z, y = place()
@@ -209,7 +209,6 @@
     for swap in swaps:
         swap.wait()
     row_terms(other)
-    pump(2)
 
     def unit(yp, w, hk, hq, masked):
         ra = 2 * w
@@ -257,8 +256,8 @@
         acc[yp, rb, 2 * hk + 1] += gv[:, 128:]
 
     def pair_at(n):
-        near = jnp.where(n == 2, 1 - 2 * odd, 2 * odd - 1)
-        return (quad + jnp.where(n == 0, 0, jnp.where(n == 1, 2, near)) + 4) % 4
+        side = jnp.where(n == 1, 2 * odd - 1, 1 - 2 * odd)
+        return (quad + jnp.where(n == 0, 0, jnp.where(n == 2, 2, side)) + 4) % 4
 
     def sum_across(zz, act):
         @pl.when(y == 0)
@@ -282,10 +281,49 @@
             src, dst = ysum_out.at[zz, 0:2], ysum_in.at[zz, 0:2]
             remote(src, dst, ysem_s.at[zz], ysem_r.at[zz], ctx=ypart).wait_recv()
 
-    def sum_home(zz):
+    def way(zz):
+        ahead = (zz - z + NZ) % NZ
+        up = (ahead <= reach[1]).astype(jnp.int32)
+        return up, jnp.where(up == 1, ahead, NZ - ahead)
+
+    def sum_hop(zz, up, at):
         return remote(
-            sum_out.at[zz], sum_in.at[z], ssend.at[zz], srecv.at[z], ctx=ctx_of(y, zz, core)
+            sum_out.at[zz], sum_in.at[up, at], ssend.at[zz], srecv.at[up, at],
+            ctx=jnp.where(up == 1, up_dev, down_dev),
         )
+
+    def sum_home(zz, up, at):
+        return remote(
+            sum_out.at[zz], home_in.at[up, at], ssend.at[zz], homer.at[up, at],
+            ctx=ctx_of(y, zz, core),
+        )
+
+    def merge(zz, up, a):
+        limit = jnp.where(up == 1, reach[1], reach[0])
+
+        @pl.when(a < limit)
+        def _():
+            sum_hop(zz, up, a).wait_recv()
+            sum_out[zz] = (acc[y, zz] + sum_in[up, a].astype(F32)).astype(BF)
+
+        @pl.when(a == limit)
+        def _():
+            sum_out[zz] = acc[y, zz].astype(BF)
+
+    def pass_far(zz):
+        up, a = way(zz)
+        merge(zz, up, a)
+        sum_hop(zz, up, a - 1).start()
+
+    def pass_mid(zz):
+        up, a = way(zz)
+        merge(zz, up, a)
+        sum_home(zz, up, a).start()
+
+    def pass_near(zz):
+        up, a = way(zz)
+        sum_out[zz] = acc[y, zz].astype(BF)
+        sum_home(zz, up, a).start()
 
     def send_across(n):
         w = pair_at(n)
@@ -301,15 +339,13 @@
         def _():
             acc[y, zz, 2:4] += ysum_in[zz, 2:4].astype(F32)
 
-    def send_home(n):
+    def far_near(n):
         w = pair_at(n)
-        for zz in (2 * w, 2 * w + 1):
-            add_across(zz)
-
-            @pl.when(zz != z)
-            def _():
-                sum_out[zz] = acc[y, zz].astype(BF)
-                sum_home(zz).start()
+        first = 2 * w
+        _, da = way(first)
+        _, db = way(first + 1)
+        flip = (da < db).astype(jnp.int32)
+        return first + flip, first + 1 - flip
 
     def weight_copies(step):
         peer = (tp + step) % TP
@@ -335,9 +371,9 @@
         return out
 
     def half_step(x, _):
-        n = jnp.where(x < 4, x // 2, 2 + x % 2)
+        n = x // 2
         w = pair_at(n)
-        far = jnp.where(x < 4, x % 2, jnp.where(x < 6, 1, 0))
+        far = jnp.where(x < 6, x % 2, 1 - x % 2)
         yp = (y + far) % 2
 
         @pl.when(far == 1)
@@ -351,6 +387,19 @@
                 copy.start()
 
         unit(yp, w, 0, 1, False)
+
+        for at, d in ((0, 2), (3, 4)):
+
+            @pl.when(x == at)
+            def _():
+                pump(d)
+
+        @pl.when(x == 7)
+        def _():
+            further, _ = far_near(2)
+            add_across(further)
+            pass_far(further)
+
         own = jnp.logical_and(far == 0, n == 0)
 
         @pl.when(own)
@@ -370,17 +419,21 @@
         def _():
             send_across(n)
 
-        for at, d in ((0, 3), (1, 4)):
-
-            @pl.when(x == at)
-            def _():
-                pump(d)
-
-        for at, done in ((3, 0), (5, 1), (6, 2), (7, 3)):
-
-            @pl.when(x == at)
-            def _():
-                send_home(done)
+        @pl.when(x == 1)
+        def _():
+            pump(3)
+
+        @pl.when(x == 3)
+        def _():
+            add_across(2 * quad)
+            add_across(2 * quad + 1)
+            pass_near(2 * quad + 1 - odd)
+
+        @pl.when(x == 5)
+        def _():
+            for zz in far_near(1):
+                add_across(zz)
+                pass_near(zz)
 
         @pl.when(x > 1)
         def _():
@@ -393,6 +446,9 @@
 
     lax.fori_loop(0, 8, half_step, 0)
 
+    _, nearer = far_near(2)
+    add_across(nearer)
+    pass_far(nearer)
     dqs[...] = (dqa[other] * SCALE).astype(BF)
     dq_copy = remote(dqs, dqr, dsem.at[0], dsem.at[1], ctx=mate)
     dq_copy.start()
@@ -400,6 +456,9 @@
         copy.wait_recv()
     for copy in weight_forwards(TP - 1):
         copy.start()
+    for zz in far_near(3):
+        add_across(zz)
+        pass_mid(zz)
     dq_copy.wait()
     for h in range(8):
         cols = slice(h * 128, (h + 1) * 128)
@@ -408,14 +467,12 @@
         dq_out[0:SPAN, cols] = jnp.where(flip16, high, low)
         dq_out[SPAN:, cols] = jnp.where(flip16, low, high)
 
-    def collect(step, _):
-        zz = z_at(step)
-        remote(sum_out.at[zz], sum_in.at[zz], ssend.at[zz], srecv.at[zz], ctx=mate).wait_recv()
-        for at in range(4):
-            acc[y, z, at] += sum_in[zz, at].astype(F32)
-        return 0
-
-    lax.fori_loop(1, NZ, collect, 0)
+    def take(up, a):
+        sum_home(z, up, a).wait_recv()
+        acc[y, z] += home_in[up, a].astype(F32)
+
+    for up, a in ((0, 1), (1, 1), (0, 2), (1, 2), (odd, 3)):
+        take(up, a)
     for out, at, factor in ((dk_out, 0, SCALE), (dv_out, 1, 1.0)):
         low = (acc[y, z, at] * factor).T.astype(BF)
         high = (acc[y, z, at + 2] * factor).T.astype(BF)
@@ -530,7 +587,7 @@
         def _():
             for copy in weight_copies(s):
                 copy.wait_send()
-            sum_home(z_at(s)).wait_send()
+            sum_hop(z_at(s), 0, 0).wait_send()
             spread(s).wait_send()
 
         for up in (0, 1):
@@ -586,7 +643,8 @@
             pltpu.VMEM((NZ,) + block, BF),
             pltpu.VMEM((NZ,) + block, BF),
             pltpu.VMEM((NZ,) + block, BF),
-            pltpu.VMEM((NZ,) + block, BF),
+            pltpu.VMEM((2, 4) + block, BF),
+            pltpu.VMEM((2, 4) + block, BF),
             pltpu.VMEM((2, 1024, 128), BF),
             pltpu.VMEM((2, 1024, 128), BF),
             pltpu.VMEM((TP, 2, FEAT, 128), BF),
@@ -609,7 +667,8 @@
             dma((NZ,)),
             dma((NZ,)),
             dma((NZ,)),
-            dma((NZ,)),
+            dma((2, 4)),
+            dma((2, 4)),
             dma((TP, 2)),
             dma((TP, 2)),
             dma((TP, 2)),

time: 98.2 us -> 93.1 us (0.948); the launches traced: 97.1 us -> 93 us
  Pallas kernels: 96.4 us -> 92.4 us
    pallas_call x1, Pallas kernels: 94.3 us -> 90.2 us  [backward(): pl.pallas_call(kernel, out_shape=[sds((256, 1024), BF), sds((256, 128), B...]
where the time goes in v4:
time: 93.1 us; the launch traced here: 93 us
  Pallas kernels  92.4 us (99%)
    pallas_call x1, Pallas kernels, backward(): pl.pallas_call(kernel, out_shape=[sds((256, 1024), BF), sds((256, 128), B...  90.2 us
    pallas_call x1, Pallas kernels, place_outputs(): pl.pallas_call(copy_kernel, out_shape=[jax.ShapeDtypeStruct(a.shape, a.dt...  2.14 us

profile of v4, /device:TPU:8, one launch (start us, length us, event | category | flops | bytes accessed | tf_op | source)
XLA Modules:
  0.0 93.0 jit_solution(2151510485243309340)
XLA Ops:
  0.6 90.2 %shard_map.145 = (bf16[256,1024]{1,0:T(8,128)(2,1)}, bf16[256,128]{1,0:T(8,128)(2,1)}, bf16[256,128]{1,0:T(8,128)(2,1)}, f32[160,128]{1,0:T(8,128)}, f32[160,128]{1,0:T(8,128)}, /*index=5*/bf16[256,640]{1,0:T(8,128)(2,1)}) custom-call(s32[64]{0:T(128)} %order.1, bf16[256,1024]{1,0:T(8,128)(2,1)} %q_hbm.1, bf16[256,128]{1,0:T(8,128)(2,1)} %k_hbm.1, ...), custom_call_target="tpu_custom_call" | custom-call | flops 12000000000 | bytes 10000000 | tf_op jit(solution)/shard_map/pallas_call | solution.py:614
  90.9 2.1 %shard_map.146 = (bf16[256,1024]{1,0:T(8,128)(2,1)}, bf16[256,128]{1,0:T(8,128)(2,1)}, bf16[256,128]{1,0:T(8,128)(2,1)}, f32[160,128]{1,0:T(8,128)}, f32[160,128]{1,0:T(8,128)}, /*index=5*/bf16[256,640]{1,0:T(8,128)(2,1)}) custom-call(bf16[256,1024]{1,0:T(8,128)(2,1)} %get-tuple-element.12.refs_0_, bf16[256,128]{1,0:T(8,128)(2,1)} %get-tuple-element.13.refs_1_, ...), custom_call_target="tpu_custom_call" | custom-call | tf_op jit(solution)/shard_map/pallas_call | solution.py:708

commit v5 on v4

--- a/solution.py
+++ b/solution.py
@@ -48,7 +48,7 @@
     order, q_hbm, k_hbm, v_hbm, o_hbm, d_hbm, ln_hbm, hid_hbm, wk, wv,
     dq_out, dk_out, dv_out, gk_out, gv_out, dh_out,
     q_in, k_in, v_in, o_in, d_in, ln_in, hid,
-    qb, db, ob, lnc, lnb, deb, dqa, kv, acc, ysum_out, ysum_in, sum_out, sum_in, home_in, dqs, dqr,
+    qb, db, ob, terms, lnb, deb, dqa, kv, acc, ysum_out, ysum_in, sum_out, sum_in, home_in, dqs, dqr,
     wbuf, dkv, gathered, part, cs, cr, gout, gin, fs, fr,
     lsem, xsend, xrecv, zsend, zrecv, ysend, yrecv, ysem_s, ysem_r, ssend, srecv, homer,
     wsend, wrecv, fsend, frecv, dsem, tsend, trecv, csend, crecv, gsend, grecv,
@@ -147,17 +147,30 @@
     for hl in range(2):
         for h in range(8):
             cols = slice(h * 128, (h + 1) * 128)
-            for full, here in ((qb, q_in), (db, d_in), (ob, o_in)):
+            for full, here in ((qb, q_in), (db, d_in)):
                 full[core, hl, cols, :] = canon(here[:SPAN, cols], here[SPAN:, cols], hl)
-    both = ln_in[...] * LOG2E
-    lnc[core, 0] = jnp.where(flip8, both[:, SPAN:], both[:, :SPAN])
-    lnc[core, 1] = jnp.where(flip8, both[:, :SPAN], both[:, SPAN:])
+            ob[hl, cols, :] = canon(o_in[:SPAN, cols], o_in[SPAN:, cols], hl)
     swaps = [
         remote(ref.at[core], ref.at[core], xsend.at[n], xrecv.at[n], ctx=mate)
-        for n, ref in enumerate((qb, db, ob, lnc))
+        for n, ref in enumerate((qb, db, terms))
     ]
-    for swap in swaps:
-        swap.start()
+    swaps[0].start()
+    swaps[1].start()
+    both = ln_in[...] * LOG2E
+    terms[core, 0, 0] = jnp.where(flip8, both[:, SPAN:], both[:, :SPAN])
+    terms[core, 1, 0] = jnp.where(flip8, both[:, :SPAN], both[:, SPAN:])
+    ones = jnp.ones((16, 128), BF)
+    head = lax.broadcasted_iota(jnp.int32, (8, 128), 0)
+    for hl in range(2):
+        prod = db[core, hl].astype(F32) * ob[hl].astype(F32)
+        high = prod.astype(BF)
+        low = (prod - high.astype(F32)).astype(BF)
+        flat = (dot(ones, high, NT) + dot(ones, low, NT))[:8, :]
+        delta = flat[:, 0:128]
+        for h in range(1, 8):
+            delta = jnp.where(head == h, flat[:, h * 128 : (h + 1) * 128], delta)
+        terms[core, hl, 1] = delta
+    swaps[2].start()
 
     def zero(n, _):
         for at in range(4):
@@ -167,28 +180,26 @@
     lax.fori_loop(0, 2 * NZ, zero, 0)
     dqa[...] = jnp.zeros_like(dqa)
 
-    ones = jnp.ones((128, 128), BF)
     head_of = lax.broadcasted_iota(jnp.int32, (32, 1024), 1) // 128
     pick = (lax.broadcasted_iota(jnp.int32, (32, 1024), 0) % 8 == head_of).astype(F32).astype(BF)
 
     def row_terms(slot):
         for hl in range(2):
-            prod = db[slot, hl].astype(F32) * ob[slot, hl].astype(F32)
-            high = prod.astype(BF)
-            low = (prod - high.astype(F32)).astype(BF)
-            deb[slot, hl] = mm(high, ones) + mm(low, ones)
-            norm = lnc[slot, hl]
-            p1 = norm.astype(BF)
-            rest = norm - p1.astype(F32)
-            p2 = rest.astype(BF)
-            rest = rest - p2.astype(F32)
-            p3 = rest.astype(BF)
-            parts = jnp.concatenate(
-                [p1.astype(F32), p2.astype(F32), p3.astype(F32), jnp.zeros((8, 128), F32)], axis=0
-            ).astype(BF)
-            wide = dot(parts, pick, TN)
-            for h in range(8):
-                lnb[slot, hl, h * 128 : (h + 1) * 128, :] = wide[:, h * 128 : (h + 1) * 128]
+            for at, wide_ref in ((0, lnb), (1, deb)):
+                term = terms[slot, hl, at]
+                p1 = term.astype(BF)
+                rest = term - p1.astype(F32)
+                p2 = rest.astype(BF)
+                rest = rest - p2.astype(F32)
+                p3 = rest.astype(BF)
+                parts = jnp.concatenate(
+                    [p1.astype(F32), p2.astype(F32), p3.astype(F32), jnp.zeros((8, 128), F32)],
+                    axis=0,
+                ).astype(BF)
+                wide = dot(parts, pick, TN)
+                for h in range(8):
+                    cols = slice(h * 128, (h + 1) * 128)
+                    wide_ref[slot, hl, cols, :] = wide[:, cols]
 
     row_terms(core)
 
@@ -326,8 +337,7 @@
         sum_home(zz, up, a).start()
 
     def send_across(n):
-        w = pair_at(n)
-        for zz in (2 * w, 2 * w + 1):
+        for zz in far_near(n):
             ysum_out[zz] = acc[1 - y, zz].astype(BF)
             sum_across(zz, lambda copy: copy.start())
 
@@ -511,13 +521,14 @@
 
         lax.fori_loop(0, NZ, fill, 0)
         swap_part(yp).start()
-    def own_part(yp, zz):
-        return part[rows_of(yp, zz, core), :] + cr[yp, zz].astype(F32)
-
-    def arm(up, a, yp):
+    def own_part(yp, zz, ch):
+        cols = slice(ch * 128, (ch + 1) * 128)
+        return part[rows_of(yp, zz, core), cols] + cr[yp, zz, :, cols].astype(F32)
+
+    def arm(up, a, q):
         return remote(
-            gout.at[up, a, yp], gin.at[up, a - 1, yp],
-            gsend.at[up, a, yp], grecv.at[up, a - 1, yp],
+            gout.at[up, a, q], gin.at[up, a - 1, q],
+            gsend.at[up, a, q], grecv.at[up, a - 1, q],
             ctx=up_dev if up else down_dev,
         )
 
@@ -530,35 +541,42 @@
             def _():
                 swap_part(yp).wait()
 
-            for up in (1, 0):
-                zz = (z + a) % NZ if up else (z - a + NZ) % NZ
-
-                @pl.when(a == reach[up])
-                def _():
-                    gout[up, a, yp] = own_part(yp, zz).astype(BF)
-
-                @pl.when(a < reach[up])
-                def _():
-                    arm(up, a + 1, yp).wait_recv()
-                    gout[up, a, yp] = (own_part(yp, zz) + gin[up, a, yp].astype(F32)).astype(BF)
-
-                @pl.when(a <= reach[up])
-                def _():
-                    arm(up, a, yp).start()
+            for ch in range(2):
+                q = yp * 2 + ch
+                for up in (1, 0):
+                    zz = (z + a) % NZ if up else (z - a + NZ) % NZ
+
+                    @pl.when(a == reach[up])
+                    def _():
+                        gout[up, a, q] = own_part(yp, zz, ch).astype(BF)
+
+                    @pl.when(a < reach[up])
+                    def _():
+                        arm(up, a + 1, q).wait_recv()
+                        mix = own_part(yp, zz, ch) + gin[up, a, q].astype(F32)
+                        gout[up, a, q] = mix.astype(BF)
+
+                    @pl.when(a <= reach[up])
+                    def _():
+                        arm(up, a, q).start()
 
         return 0
 
     lax.fori_loop(0, 4, arms, 0)
 
-    def plane_sum(yp):
-        arm(1, 1, yp).wait_recv()
-        arm(0, 1, yp).wait_recv()
-        return own_part(yp, z) + gin[1, 0, yp].astype(F32) + gin[0, 0, yp].astype(F32)
-
-    fs[...] = plane_sum(1 - y).astype(BF)
-    f_copy = remote(fs, fr, dsem.at[2], dsem.at[3], ctx=ypart)
-    f_copy.start()
-    final = plane_sum(y)
+    def plane_sum(yp, ch):
+        q = yp * 2 + ch
+        arm(1, 1, q).wait_recv()
+        arm(0, 1, q).wait_recv()
+        return own_part(yp, z, ch) + gin[1, 0, q].astype(F32) + gin[0, 0, q].astype(F32)
+
+    f_copies = []
+    for ch in range(2):
+        fs[ch] = plane_sum(1 - y, ch).astype(BF)
+        f_copies.append(
+            remote(fs.at[ch], fr.at[ch], dsem.at[2 + 2 * ch], dsem.at[3 + 2 * ch], ctx=ypart)
+        )
+        f_copies[ch].start()
 
     gathered[tp] = mine
     loads[7].wait()
@@ -574,10 +592,10 @@
         total = term if total is None else total + term
     dh_out[...] = total.astype(BF)
 
-    f_copy.wait()
-    final = final + fr[...].astype(F32)
-    gk_out[...] = final[:, :128]
-    gv_out[...] = final[:, 128:]
+    for ch, out in ((0, gk_out), (1, gv_out)):
+        mine_sum = plane_sum(y, ch)
+        f_copies[ch].wait()
+        out[...] = mine_sum + fr[ch].astype(F32)
 
     def drain(s, _):
         across(s, lambda copy: copy.wait_send())
@@ -595,8 +613,8 @@
             @pl.when(s < reach[up])
             def _():
                 hop(up, s).wait_send()
-                for yp in range(2):
-                    arm(up, s + 1, yp).wait_send()
+                for q in range(4):
+                    arm(up, s + 1, q).wait_send()
 
         return 0
 
@@ -633,8 +651,8 @@
             pltpu.VMEM((256, 5120), BF),
             pltpu.VMEM(rows, BF),
             pltpu.VMEM(rows, BF),
-            pltpu.VMEM(rows, BF),
-            pltpu.VMEM((2, 2, 8, 128), F32),
+            pltpu.VMEM((2, 1024, 128), BF),
+            pltpu.VMEM((2, 2, 2, 8, 128), F32),
             pltpu.VMEM(rows, F32),
             pltpu.VMEM(rows, F32),
             pltpu.VMEM(rows, F32),
@@ -653,10 +671,10 @@
             pltpu.VMEM((5120, 256), F32),
             pltpu.VMEM((2, NZ) + piece, BF),
             pltpu.VMEM((2, NZ) + piece, BF),
-            pltpu.VMEM((2, 5, 2) + piece, BF),
-            pltpu.VMEM((2, 4, 2) + piece, BF),
-            pltpu.VMEM(piece, BF),
-            pltpu.VMEM(piece, BF),
+            pltpu.VMEM((2, 5, 4, WROWS, 128), BF),
+            pltpu.VMEM((2, 4, 4, WROWS, 128), BF),
+            pltpu.VMEM((2, WROWS, 128), BF),
+            pltpu.VMEM((2, WROWS, 128), BF),
             dma((9,)),
             dma((4,)),
             dma((4,)),
@@ -673,13 +691,13 @@
             dma((TP, 2)),
             dma((TP, 2)),
             dma((TP, 2)),
-            dma((4,)),
+            dma((6,)),
             dma((TP,)),
             dma((TP,)),
             dma((2,)),
             dma((2,)),
-            dma((2, 5, 2)),
-            dma((2, 5, 2)),
+            dma((2, 5, 4)),
+            dma((2, 5, 4)),
         ],
         compiler_params=pltpu.CompilerParams(
             collective_id=0, has_side_effects=True, vmem_limit_bytes=58 * 2**20

time: 93.1 us -> 90.4 us (0.971)
  Pallas kernels: 92.4 us -> 89.5 us
    pallas_call x1, Pallas kernels: 90.2 us -> 87.3 us  [backward(): pl.pallas_call(kernel, out_shape=[sds((256, 1024), BF), sds((256, 128), B...]
where the time goes in v5:
time: 90.4 us; the launch traced here: 90.1 us
  Pallas kernels  89.5 us (99%)
    pallas_call x1, Pallas kernels, backward(): pl.pallas_call(kernel, out_shape=[sds((256, 1024), BF), sds((256, 128), B...  87.3 us
    pallas_call x1, Pallas kernels, place_outputs(): pl.pallas_call(copy_kernel, out_shape=[jax.ShapeDtypeStruct(a.shape, a.dt...  2.14 us

profile of v5, /device:TPU:8, one launch (start us, length us, event | category | flops | bytes accessed | tf_op | source)
XLA Modules:
  0.0 90.1 jit_solution(6589418163146990642)
XLA Ops:
  0.6 87.3 %shard_map.145 = (bf16[256,1024]{1,0:T(8,128)(2,1)}, bf16[256,128]{1,0:T(8,128)(2,1)}, bf16[256,128]{1,0:T(8,128)(2,1)}, f32[160,128]{1,0:T(8,128)}, f32[160,128]{1,0:T(8,128)}, /*index=5*/bf16[256,640]{1,0:T(8,128)(2,1)}) custom-call(s32[64]{0:T(128)} %order.1, bf16[256,1024]{1,0:T(8,128)(2,1)} %q_hbm.1, bf16[256,128]{1,0:T(8,128)(2,1)} %k_hbm.1, ...), custom_call_target="tpu_custom_call" | custom-call | flops 12000000000 | bytes 10000000 | tf_op jit(solution)/shard_map/pallas_call | solution.py:632
  88.0 2.1 %shard_map.146 = (bf16[256,1024]{1,0:T(8,128)(2,1)}, bf16[256,128]{1,0:T(8,128)(2,1)}, bf16[256,128]{1,0:T(8,128)(2,1)}, f32[160,128]{1,0:T(8,128)}, f32[160,128]{1,0:T(8,128)}, /*index=5*/bf16[256,640]{1,0:T(8,128)(2,1)}) custom-call(bf16[256,1024]{1,0:T(8,128)(2,1)} %get-tuple-element.12.refs_0_, bf16[256,128]{1,0:T(8,128)(2,1)} %get-tuple-element.13.refs_1_, ...), custom_call_target="tpu_custom_call" | custom-call | tf_op jit(solution)/shard_map/pallas_call | solution.py:726

commit v6 on v5

--- a/solution.py
+++ b/solution.py
@@ -270,84 +270,94 @@
         side = jnp.where(n == 1, 2 * odd - 1, 1 - 2 * odd)
         return (quad + jnp.where(n == 0, 0, jnp.where(n == 2, 2, side)) + 4) % 4
 
+    def half(ref, p):
+        return ref.at[2 * p : 2 * p + 2]
+
+    def sum_y(zz, p):
+        return remote(
+            half(ysum_out.at[zz], p), half(ysum_in.at[zz], p),
+            ysem_s.at[zz, p], ysem_r.at[zz, p], ctx=ypart,
+        )
+
     def sum_across(zz, act):
+        act(sum_y(zz, 0))
+
         @pl.when(y == 0)
         def _():
-            act(remote(ysum_out.at[zz], ysum_in.at[zz], ysem_s.at[zz], ysem_r.at[zz], ctx=ypart))
-
-        @pl.when(y == 1)
-        def _():
-            src, dst = ysum_out.at[zz, 0:2], ysum_in.at[zz, 0:2]
-            act(remote(src, dst, ysem_s.at[zz], ysem_r.at[zz], ctx=ypart))
-
-    def sum_across_wait(zz):
-        @pl.when(y == 1)
-        def _():
-            remote(
-                ysum_out.at[zz], ysum_in.at[zz], ysem_s.at[zz], ysem_r.at[zz], ctx=ypart
-            ).wait_recv()
-
-        @pl.when(y == 0)
-        def _():
-            src, dst = ysum_out.at[zz, 0:2], ysum_in.at[zz, 0:2]
-            remote(src, dst, ysem_s.at[zz], ysem_r.at[zz], ctx=ypart).wait_recv()
+            act(sum_y(zz, 1))
 
     def way(zz):
         ahead = (zz - z + NZ) % NZ
         up = (ahead <= reach[1]).astype(jnp.int32)
         return up, jnp.where(up == 1, ahead, NZ - ahead)
 
-    def sum_hop(zz, up, at):
+    def sum_hop(zz, up, at, p):
         return remote(
-            sum_out.at[zz], sum_in.at[up, at], ssend.at[zz], srecv.at[up, at],
+            half(sum_out.at[zz], p), half(sum_in.at[up, at], p),
+            ssend.at[zz, p], srecv.at[up, at, p],
             ctx=jnp.where(up == 1, up_dev, down_dev),
         )
 
-    def sum_home(zz, up, at):
+    def sum_home(zz, up, at, p):
         return remote(
-            sum_out.at[zz], home_in.at[up, at], ssend.at[zz], homer.at[up, at],
-            ctx=ctx_of(y, zz, core),
+            half(sum_out.at[zz], p), half(home_in.at[up, at], p),
+            ssend.at[zz, p], homer.at[up, at, p], ctx=ctx_of(y, zz, core),
         )
 
-    def merge(zz, up, a):
+    def merge(zz, up, a, p):
         limit = jnp.where(up == 1, reach[1], reach[0])
+        at = slice(2 * p, 2 * p + 2)
 
         @pl.when(a < limit)
         def _():
-            sum_hop(zz, up, a).wait_recv()
-            sum_out[zz] = (acc[y, zz] + sum_in[up, a].astype(F32)).astype(BF)
+            sum_hop(zz, up, a, p).wait_recv()
+            sum_out[zz, at] = (acc[y, zz, at] + sum_in[up, a, at].astype(F32)).astype(BF)
 
         @pl.when(a == limit)
         def _():
-            sum_out[zz] = acc[y, zz].astype(BF)
+            sum_out[zz, at] = acc[y, zz, at].astype(BF)
 
     def pass_far(zz):
         up, a = way(zz)
-        merge(zz, up, a)
-        sum_hop(zz, up, a - 1).start()
+        for p in range(2):
+            add_half(zz, p)
+            merge(zz, up, a, p)
+            sum_hop(zz, up, a - 1, p).start()
 
     def pass_mid(zz):
         up, a = way(zz)
-        merge(zz, up, a)
-        sum_home(zz, up, a).start()
+        for p in range(2):
+            add_half(zz, p)
+            merge(zz, up, a, p)
+            sum_home(zz, up, a, p).start()
 
     def pass_near(zz):
         up, a = way(zz)
-        sum_out[zz] = acc[y, zz].astype(BF)
-        sum_home(zz, up, a).start()
+        for p in range(2):
+            add_half(zz, p)
+            at = slice(2 * p, 2 * p + 2)
+            sum_out[zz, at] = acc[y, zz, at].astype(BF)
+            sum_home(zz, up, a, p).start()
 
     def send_across(n):
         for zz in far_near(n):
             ysum_out[zz] = acc[1 - y, zz].astype(BF)
             sum_across(zz, lambda copy: copy.start())
 
+    def add_half(zz, p):
+        def add():
+            sum_y(zz, p).wait_recv()
+            at = slice(2 * p, 2 * p + 2)
+            acc[y, zz, at] += ysum_in[zz, at].astype(F32)
+
+        if p == 0:
+            add()
+        else:
+            pl.when(y == 1)(add)
+
     def add_across(zz):
-        sum_across_wait(zz)
-        acc[y, zz, 0:2] += ysum_in[zz, 0:2].astype(F32)
-
-        @pl.when(y == 1)
-        def _():
-            acc[y, zz, 2:4] += ysum_in[zz, 2:4].astype(F32)
+        add_half(zz, 0)
+        add_half(zz, 1)
 
     def far_near(n):
         w = pair_at(n)
@@ -407,7 +417,6 @@
         @pl.when(x == 7)
         def _():
             further, _ = far_near(2)
-            add_across(further)
             pass_far(further)
 
         own = jnp.logical_and(far == 0, n == 0)
@@ -435,14 +444,12 @@
 
         @pl.when(x == 3)
         def _():
-            add_across(2 * quad)
-            add_across(2 * quad + 1)
+            add_across(z)
             pass_near(2 * quad + 1 - odd)
 
         @pl.when(x == 5)
         def _():
             for zz in far_near(1):
-                add_across(zz)
                 pass_near(zz)
 
         @pl.when(x > 1)
@@ -457,7 +464,6 @@
     lax.fori_loop(0, 8, half_step, 0)
 
     _, nearer = far_near(2)
-    add_across(nearer)
     pass_far(nearer)
     dqs[...] = (dqa[other] * SCALE).astype(BF)
     dq_copy = remote(dqs, dqr, dsem.at[0], dsem.at[1], ctx=mate)
@@ -467,7 +473,6 @@
     for copy in weight_forwards(TP - 1):
         copy.start()
     for zz in far_near(3):
-        add_across(zz)
         pass_mid(zz)
     dq_copy.wait()
     for h in range(8):
@@ -478,7 +483,8 @@
         dq_out[SPAN:, cols] = jnp.where(flip16, low, high)
 
     def take(up, a):
-        sum_home(z, up, a).wait_recv()
+        for p in range(2):
+            sum_home(z, up, a, p).wait_recv()
         acc[y, z] += home_in[up, a].astype(F32)
 
     for up, a in ((0, 1), (1, 1), (0, 2), (1, 2), (odd, 3)):
@@ -605,7 +611,8 @@
         def _():
             for copy in weight_copies(s):
                 copy.wait_send()
-            sum_hop(z_at(s), 0, 0).wait_send()
+            for p in range(2):
+                sum_hop(z_at(s), 0, 0, p).wait_send()
             spread(s).wait_send()
 
         for up in (0, 1):
@@ -682,11 +689,11 @@
             dma((2, 5)),
             dma((NZ,)),
             dma((NZ,)),
-            dma((NZ,)),
-            dma((NZ,)),
-            dma((NZ,)),
-            dma((2, 4)),
-            dma((2, 4)),
+            dma((NZ, 2)),
+            dma((NZ, 2)),
+            dma((NZ, 2)),
+            dma((2, 4, 2)),
+            dma((2, 4, 2)),
             dma((TP, 2)),
             dma((TP, 2)),
             dma((TP, 2)),

time: 90.4 us -> 89.2 us (0.987)
  Pallas kernels: 89.5 us -> 88.2 us
    pallas_call x1, Pallas kernels: 87.3 us -> 86 us  [backward(): pl.pallas_call(kernel, out_shape=[sds((256, 1024), BF), sds((256, 128), B...]
where the time goes in v6:
time: 89.2 us; the launch traced here: 88.8 us
  Pallas kernels  88.2 us (99%)
    pallas_call x1, Pallas kernels, backward(): pl.pallas_call(kernel, out_shape=[sds((256, 1024), BF), sds((256, 128), B...  86 us
    pallas_call x1, Pallas kernels, place_outputs(): pl.pallas_call(copy_kernel, out_shape=[jax.ShapeDtypeStruct(a.shape, a.dt...  2.14 us

profile of v6, /device:TPU:8, one launch (start us, length us, event | category | flops | bytes accessed | tf_op | source)
XLA Modules:
  0.0 88.8 jit_solution(5250454516667067064)
XLA Ops:
  0.6 86.0 %shard_map.145 = (bf16[256,1024]{1,0:T(8,128)(2,1)}, bf16[256,128]{1,0:T(8,128)(2,1)}, bf16[256,128]{1,0:T(8,128)(2,1)}, f32[160,128]{1,0:T(8,128)}, f32[160,128]{1,0:T(8,128)}, /*index=5*/bf16[256,640]{1,0:T(8,128)(2,1)}) custom-call(s32[64]{0:T(128)} %order.1, bf16[256,1024]{1,0:T(8,128)(2,1)} %q_hbm.1, bf16[256,128]{1,0:T(8,128)(2,1)} %k_hbm.1, ...), custom_call_target="tpu_custom_call" | custom-call | flops 12000000000 | bytes 10000000 | tf_op jit(solution)/shard_map/pallas_call | solution.py:639
  86.7 2.1 %shard_map.146 = (bf16[256,1024]{1,0:T(8,128)(2,1)}, bf16[256,128]{1,0:T(8,128)(2,1)}, bf16[256,128]{1,0:T(8,128)(2,1)}, f32[160,128]{1,0:T(8,128)}, f32[160,128]{1,0:T(8,128)}, /*index=5*/bf16[256,640]{1,0:T(8,128)(2,1)}) custom-call(bf16[256,1024]{1,0:T(8,128)(2,1)} %get-tuple-element.12.refs_0_, bf16[256,128]{1,0:T(8,128)(2,1)} %get-tuple-element.13.refs_1_, ...), custom_call_target="tpu_custom_call" | custom-call | tf_op jit(solution)/shard_map/pallas_call | solution.py:733
